TPU v7x, 32 devices: a whole 2x2x4 slice. The times are simulated.
32 devices in a mesh: dp: 8 (over z, y), mp: 4 (over x, core).
Axes of the slice: x: 2, y: 2, z: 4, core: 2. Of those that a mesh axis runs over, the one named last changes fastest.
Arguments:
- tokens: bfloat16 [16384, 1024], P(('dp', 'mp')), may hold values from -6 to 6
- cotangent: bfloat16 [16384, 1024], P(('dp', 'mp')), may hold values from -6 to 6
- item_lengths: int32 [40], P('dp'), may hold values from 0 to 1024, as said below
- gsd_ratio: float32 [40], P('dp'), may hold values from 0.25 to 1
- ln1_gain: bfloat16 [1024], replicated, may hold values from 0.5 to 1.5
- ln1_bias: bfloat16 [1024], replicated, may hold values from -1.1953125 to 1.1953125
- w_qkv: bfloat16 [3, 1024, 1024], P(None, 'mp'), may hold values from -0.1875 to 0.1875
- qv_bias: float32 [2, 1024], P(None, 'mp'), may hold values from -3 to 3
- w_out: bfloat16 [1024, 1024], P('mp'), may hold values from -1.5 to 1.5
- out_bias: float32 [1024], replicated, may hold values from -1.2 to 1.2
- ln2_gain: float32 [1024], replicated, may hold values from 0.5 to 1.5
- ln2_bias: float32 [1024], replicated, may hold values from -1.2 to 1.2
- w_up: bfloat16 [1024, 4096], P(None, 'mp'), may hold values from -0.1875 to 0.1875
- up_bias: float32 [4096], P('mp'), may hold values from -1.8 to 1.8
- w_down: bfloat16 [4096, 1024], P('mp'), may hold values from -0.09375 to 0.09375
- down_bias: float32 [1024], replicated, may hold values from -1.2 to 1.2
Outputs:
- output: bfloat16 [16384, 1024], P(('dp', 'mp'))
- input_grad: float32 [16384, 1024], P(('dp', 'mp'))
- grad_ln1_gain: float32 [1024], replicated
- grad_ln1_bias: float32 [1024], replicated
- grad_qkv: float32 [3, 1024, 1024], P(None, 'mp')
- grad_qv_bias: float32 [2, 1024], P(None, 'mp')
- grad_out_weight: float32 [1024, 1024], P('mp')
- grad_out_bias: float32 [1024], replicated
- grad_ln2_gain: float32 [1024], replicated
- grad_ln2_bias: float32 [1024], replicated
- grad_up: float32 [1024, 4096], P(None, 'mp')
- grad_up_bias: float32 [4096], P('mp')
- grad_down: float32 [4096, 1024], P('mp')
- grad_down_bias: float32 [1024], replicated
- stats: float32 [3], replicated
Inputs may be any that keep to these rules, and one draw needn't show every extreme that they name: `item_lengths`: in each block of 5 entries the first is a scene of 512 to 1024 patches, exactly 1024 in some block of every draw; the others are chips of 64 to 256 patches, nonzero ones first, then zeros; the items of a block fit in its 2048 rows and the rows after them are padding.
All inputs are finite; a program needn't handle non-finite values.
Results may differ from a plain program's by a relative error of at most 0.02.
Values may be sent and summed in bfloat16 or wider, within the bound.
No kernel may reach another device: no remote copies, remote signals or barrier semaphores. Data moves between devices by JAX's collectives and lax.ppermute only.
A program may use at most 192 MiB of HBM per device.

v0:
```python
import functools
import math

import jax
import jax.numpy as jnp
import numpy as np
from jax import lax
from jax.experimental import pallas as pl
from jax.experimental.pallas import tpu as pltpu
from jax.sharding import PartitionSpec as P

HD = 64
EPS = 1e-06
MASKED = -1e30
F32 = jnp.float32
BF16 = jnp.bfloat16
NT = (((1,), (1,)), ((), ()))
TN = (((0,), (0,)), ((), ()))
NN = (((1,), (0,)), ((), ()))


def mxu(left, right, dims):
    return lax.dot_general(left, right, dims, preferred_element_type=F32)


def whole(shape):
    return pl.BlockSpec(shape, lambda *_: (0,) * len(shape))


def scalars():
    return pl.BlockSpec(memory_space=pltpu.SMEM)


def call(body, grid, in_specs, out_specs, out_shape, flops, moved, scratch=(), limit=12):
    return pl.pallas_call(
        body,
        grid=grid,
        in_specs=in_specs,
        out_specs=out_specs,
        out_shape=out_shape,
        scratch_shapes=list(scratch),
        compiler_params=pltpu.CompilerParams(
            dimension_semantics=("arbitrary",) * len(grid), vmem_limit_bytes=limit * 1024 * 1024
        ),
        cost_estimate=pl.CostEstimate(
            flops=0, bytes_accessed=0, transcendentals=0
        ),
    )


def like(shape, dtype):
    return jax.ShapeDtypeStruct(shape, dtype)


def item_ends(lengths_ref, item_count):
    ends, total = [], 0
    for item in range(item_count):
        total = total + lengths_ref[item]
        ends.append(total)
    return ends


def segment_of(rows, ends):
    segment = jnp.zeros(rows.shape, jnp.int32)
    for end in ends:
        segment = segment + jnp.where(rows >= end, 1, 0)
    return segment


def scalar_segment(row, ends):
    segment = jnp.int32(0)
    for end in ends:
        segment = segment + jnp.where(row >= end, 1, 0)
    return segment


def valid_column(lengths_ref, item_count, first_row, row_count):
    rows = first_row + lax.broadcasted_iota(jnp.int32, (row_count, 1), 0)
    return jnp.where(rows < item_ends(lengths_ref, item_count)[-1], 1.0, 0.0).astype(F32)


def normalize(stream):
    centred = stream - jnp.mean(stream, axis=1, keepdims=True)
    rstd = lax.rsqrt(jnp.mean(centred * centred, axis=1, keepdims=True) + EPS)
    return centred * rstd, rstd


def norm_back(gradient, scaled, gain, rstd):
    spread = gradient * gain
    first = jnp.mean(spread, axis=1, keepdims=True)
    second = jnp.mean(spread * scaled, axis=1, keepdims=True)
    return rstd * (spread - first - scaled * second)


def column_sum(array):
    return jnp.sum(array, axis=0, keepdims=True)


def sin_cos(angle):
    turns = jnp.floor(angle * (2.0 / math.pi) + 0.5)
    rest = angle - turns * 1.5703125
    rest = rest - turns * 4.837512969970703125e-4
    rest = rest - turns * 7.54978995489188216e-8
    square = rest * rest
    sine = rest + rest * square * (
        -1.6666654611e-1 + square * (8.3321608736e-3 + square * -1.9515295891e-4)
    )
    cosine = (
        1.0
        - 0.5 * square
        + square
        * square
        * (
            4.166664568298827e-2
            + square * (-1.388731625493765e-3 + square * 2.443315711809948e-5)
        )
    )
    quarter = turns.astype(jnp.int32)
    odd = (quarter & 1) == 1
    sine_flip = (quarter & 2) != 0
    cosine_flip = ((quarter + 1) & 2) != 0
    first = jnp.where(odd, cosine, sine)
    second = jnp.where(odd, sine, cosine)
    return jnp.where(sine_flip, -first, first), jnp.where(cosine_flip, -second, second)


def encode_body(item_count, lengths, ratios, place, tokens, freq, gain, bias, stream_out, normed_out):
    rows_here, width = tokens.shape
    row = (
        place[0] * (rows_here * pl.num_programs(0))
        + pl.program_id(0) * rows_here
        + lax.broadcasted_iota(jnp.int32, (rows_here, 1), 0)
    )
    position = jnp.zeros((rows_here, 1), jnp.int32)
    ratio = jnp.zeros((rows_here, 1), F32)
    start = 0
    for item in range(item_count):
        end = start + lengths[item]
        inside = (row >= start) & (row < end)
        position = jnp.where(inside, row - start, position)
        ratio = jnp.where(inside, ratios[item], ratio)
        start = end
    angle = (position.astype(F32) * ratio) * freq[...]
    sine, cosine = sin_cos(angle)
    stream = tokens[...].astype(F32) + jnp.concatenate([sine, cosine], axis=1)
    stream_out[...] = stream
    scaled, _ = normalize(stream)
    normed_out[...] = (scaled * gain[...].astype(F32) + bias[...].astype(F32)).astype(BF16)


def encode(lengths, ratios, place, tokens, gain, bias):
    rows, width = tokens.shape
    half = width // 2
    tile = min(128, rows)
    freq = np.exp(np.arange(half) * (-math.log(10000.0) / half)).astype(np.float32)[None]
    body = functools.partial(encode_body, lengths.shape[0])
    block = pl.BlockSpec((tile, width), lambda i: (i, 0))
    return call(
        body,
        (rows // tile,),
        [scalars(), scalars(), scalars(), block, whole((1, half)), whole((1, width)), whole((1, width))],
        [block, block],
        [like((rows, width), F32), like((rows, width), BF16)],
        60 * rows * width,
        8 * rows * width,
    )(lengths, ratios, place, tokens, freq, gain, bias)


def mask_body(item_count, lengths, place, cotangent, out):
    rows = cotangent.shape[0]
    valid = valid_column(lengths, item_count, place[0] * rows, rows)
    out[...] = (valid * cotangent[...].astype(F32)).astype(BF16)


def mask_rows(lengths, place, cotangent):
    return call(
        functools.partial(mask_body, lengths.shape[0]),
        (1,),
        [scalars(), scalars(), whole(cotangent.shape)],
        whole(cotangent.shape),
        like(cotangent.shape, BF16),
        2 * cotangent.size,
        4 * cotangent.size,
    )(lengths, place, cotangent)


def local_tile(tile, tile_rows, own_rows, place):
    return tile ^ ((place * own_rows) // tile_rows)


def first_and_last(tile, tile_rows, other_rows, ends):
    low = scalar_segment(tile * tile_rows, ends)
    high = scalar_segment(tile * tile_rows + tile_rows - 1, ends)
    start, stop = jnp.int32(0), jnp.int32(0)
    for item, end in enumerate(ends):
        start = jnp.where(low > item, end, start)
        stop = jnp.where(high >= item, end, stop)
    return start // other_rows, (stop - 1) // other_rows


def used_tiles(tile_rows, ends):
    return (ends[-1] + tile_rows - 1) // tile_rows


def head_lanes(count):
    lane = lax.broadcasted_iota(jnp.int32, (1, 2 * HD), 1)
    return [jnp.where(lane // HD == k, 1.0, 0.0) for k in range(count)]


def marks(tile, tile_rows, own_rows, place, ends):
    rows = tile * tile_rows + lax.broadcasted_iota(jnp.int32, (tile_rows, 2 * HD), 0)
    lane = lax.broadcasted_iota(jnp.int32, (tile_rows, 2 * HD), 1) % HD
    same = segment_of(rows ^ (place * own_rows), ends) == lane
    query_marks = jnp.where(same, 1.0, 0.0)
    key_marks = jnp.where(same | (lane > len(ends)), 0.0, MASKED)
    return query_marks, key_marks


class Rows:
    def __init__(self, tile_rows, own_rows):
        self.part = min(tile_rows, own_rows)
        self.tile_rows, self.own_rows = tile_rows, own_rows

    def pair(self, refs, tile, column, count):
        found = []
        for row in range(tile * self.tile_rows, (tile + 1) * self.tile_rows, self.part):
            ref = refs[row // self.own_rows]
            found.append(ref[pl.ds(row % self.own_rows, self.part), column : column + count * HD])
        found = found[0] if len(found) == 1 else jnp.concatenate(found, axis=0)
        if count == 1:
            found = jnp.concatenate([found, jnp.zeros_like(found)], axis=1)
        return found


def attend_body(item_count, heads, tile_q, tile, piece_count, lengths, place_ref, *refs):
    pieces = refs[:piece_count]
    out, lse_out = refs[piece_count : piece_count + 2]
    qa, ka, vt, acc, top = refs[piece_count + 2 :]
    own_rows = pieces[0].shape[0]
    tiles = own_rows * piece_count // tile
    ratio = tile_q // tile
    width = heads * HD
    place = place_ref[0]
    ends = item_ends(lengths, item_count)
    rows = Rows(tile, own_rows)
    lanes = head_lanes(2)
    for t in range(tiles):
        query_marks, key_marks = marks(t, tile, own_rows, place, ends)
        here = slice(t % ratio * tile, (t % ratio + 1) * tile)
        for h in range(0, heads, 2):
            count = min(2, heads - h)
            query = rows.pair(pieces, t, h * HD, count)
            key = rows.pair(pieces, t, width + h * HD, count)
            value = rows.pair(pieces, t, 2 * width + h * HD, count).T
            for k in range(count):
                mine, other = lanes[k], lanes[1 - k]
                scale = (mine * HD**-0.5).astype(BF16)
                qa[h + k, t // ratio, here] = query * scale + (query_marks * other).astype(BF16)
                ka[h + k, t] = key * mine.astype(BF16) + (key_marks * other).astype(BF16)
                vt[h + k, t, :HD] = value[k * HD : (k + 1) * HD]
                vt[h + k, t, HD:] = jnp.ones((vt.shape[2] - HD, tile), BF16)

    def query_tile(tile_index, carry):
        i = local_tile(tile_index, tile_q, own_rows, place)
        first, last = first_and_last(tile_index, tile_q, tile, ends)
        acc[...] = jnp.zeros(acc.shape, F32)
        top[...] = jnp.full(top.shape, -3e38, F32)

        def key_tile(other_index, inner):
            j = local_tile(other_index, tile, own_rows, place)
            scores = [mxu(ka[h, j], qa[h, i], NT) for h in range(heads)]
            old = [top[h] for h in range(heads)]
            new = [jnp.maximum(old[h], jnp.max(scores[h], axis=0, keepdims=True)) for h in range(heads)]
            probs = [jnp.exp(scores[h] - new[h]).astype(BF16) for h in range(heads)]
            mixed = [mxu(vt[h, j], probs[h], NN) for h in range(heads)]
            for h in range(heads):
                top[h] = new[h]
                acc[h] = acc[h] * jnp.exp(old[h] - new[h]) + mixed[h]
            return inner

        lax.fori_loop(first, last + 1, key_tile, 0)
        here = pl.ds(pl.multiple_of(i * tile_q, tile_q), tile_q)
        for h in range(0, heads, 2):
            count = min(2, heads - h)
            mixed = []
            for k in range(count):
                total = acc[h + k, HD : HD + 1, :]
                lse = top[h + k] + jnp.log(total)
                for s in range(ratio):
                    lse_out[h + k, i * ratio + s] = lse[:, s * tile : (s + 1) * tile]
                mixed.append(acc[h + k, :HD, :] / total)
            mixed = jnp.concatenate(mixed, axis=0) if count > 1 else mixed[0]
            out[here, h * HD : (h + count) * HD] = mixed.T.astype(BF16)
        return carry

    def unused_tile(tile_index, carry):
        i = local_tile(tile_index, tile_q, own_rows, place)
        for s in range(ratio):
            lse_out[:, i * ratio + s] = jnp.zeros((heads, 1, tile), F32)
        out[pl.ds(pl.multiple_of(i * tile_q, tile_q), tile_q), :] = jnp.zeros((tile_q, width), BF16)
        return carry

    used = used_tiles(tile_q, ends)
    lax.fori_loop(0, used, query_tile, 0)
    lax.fori_loop(used, tiles // ratio, unused_tile, 0)


def attend(lengths, place, pieces):
    own_rows, width3 = pieces[0].shape
    width = width3 // 3
    heads = width // HD
    rows = own_rows * len(pieces)
    tile = min(256, rows)
    tile_q = min(512, rows)
    tiles = rows // tile
    body = functools.partial(attend_body, lengths.shape[0], heads, tile_q, tile, len(pieces))
    return call(
        body,
        (1,),
        [scalars(), scalars()] + [whole((own_rows, width3))] * len(pieces),
        [whole((rows, width)), whole((heads, tiles, 1, tile))],
        [like((rows, width), BF16), like((heads, tiles, 1, tile), F32)],
        rows * rows * width * 2,
        10 * rows * width,
        [
            pltpu.VMEM((heads, rows // tile_q, tile_q, 2 * HD), BF16),
            pltpu.VMEM((heads, tiles, tile, 2 * HD), BF16),
            pltpu.VMEM((heads, tiles, HD + 16, tile), BF16),
            pltpu.VMEM((heads, HD + 16, tile_q), F32),
            pltpu.VMEM((heads, 1, tile_q), F32),
        ],
        limit=20,
    )(lengths, place, *pieces)


def attend_back_body(item_count, start, heads, tile, piece_count, lengths, place_ref, *refs):
    pieces = refs[:piece_count]
    grads = refs[piece_count : 2 * piece_count]
    mixed, lse, out, sums = refs[2 * piece_count : 2 * piece_count + 4]
    qa, qm, ka, kt, vals, dos, delta, dk, dv, dqt = refs[2 * piece_count + 4 :]
    own_rows = pieces[0].shape[0]
    tiles = own_rows * piece_count // tile
    width = heads * HD
    full = pieces[0].shape[1] // 3
    base = start * HD
    place = place_ref[0]
    ends = item_ends(lengths, item_count)
    rows = Rows(tile, own_rows)
    lanes = head_lanes(2)
    scale = HD**-0.5
    for t in range(tiles):
        query_marks, key_marks = marks(t, tile, own_rows, place, ends)
        for h in range(0, heads, 2):
            count = min(2, heads - h)
            column = base + h * HD
            query = rows.pair(pieces, t, column, count)
            key = rows.pair(pieces, t, full + column, count)
            grad = rows.pair(grads, t, column, count)
            came = mixed[t * tile : (t + 1) * tile, column : column + count * HD].astype(F32)
            if count == 1:
                came = jnp.concatenate([came, jnp.zeros_like(came)], axis=1)
            weighed = (grad.astype(F32) * came).T
            turned = key.T
            vals[h // 2, t] = rows.pair(pieces, t, 2 * full + column, count)
            for k in range(count):
                mine, other = lanes[k], lanes[1 - k]
                alone = query * (mine * scale).astype(BF16)
                qm[h + k, t] = alone
                qa[h + k, t] = alone + (query_marks * other).astype(BF16)
                ka[h + k, t] = key * mine.astype(BF16) + (key_marks * other).astype(BF16)
                dos[h + k, t] = grad * mine.astype(BF16)
                kt[h + k, t] = turned[k * HD : (k + 1) * HD]
                delta[h + k, t] = column_sum(weighed[k * HD : (k + 1) * HD])
    dqt[...] = jnp.zeros(dqt.shape, F32)

    def key_tile(tile_index, carry):
        j = local_tile(tile_index, tile, own_rows, place)
        first, last = first_and_last(tile_index, tile, tile, ends)
        dk[...] = jnp.zeros(dk.shape, F32)
        dv[...] = jnp.zeros(dv.shape, F32)

        def query_tile(other_index, inner):
            i = local_tile(other_index, tile, own_rows, place)
            scores = [mxu(ka[h, j], qa[h, i], NT) for h in range(heads)]
            grad_probs = [mxu(vals[h // 2, j], dos[h, i], NT) for h in range(heads)]
            for h in range(heads):
                probs = jnp.exp(scores[h] - lse[start + h, i])
                grad_scores = (probs * (grad_probs[h] - delta[h, i])).astype(BF16)
                dv[h] += mxu(probs.astype(BF16), dos[h, i], NN)
                dk[h] += mxu(grad_scores, qm[h, i], NN)
                dqt[h, i] += mxu(kt[h, j], grad_scores, NN)
            return inner

        lax.fori_loop(first, last + 1, query_tile, 0)
        here = pl.ds(pl.multiple_of(j * tile, tile), tile)
        for h in range(0, heads, 2):
            count = min(2, heads - h)
            first = width + h * HD
            for kept, column in ((dk, first), (dv, width + first)):
                both = kept[h] + kept[h + 1] if count > 1 else kept[h]
                out[here, column : column + count * HD] = both[:, : count * HD].astype(BF16)
        return carry

    def unused_tile(tile_index, carry):
        j = local_tile(tile_index, tile, own_rows, place)
        here = pl.ds(pl.multiple_of(j * tile, tile), tile)
        out[here, width:] = jnp.zeros((tile, 2 * width), BF16)
        return carry

    used = used_tiles(tile, ends)
    lax.fori_loop(0, used, key_tile, 0)
    lax.fori_loop(used, tiles, unused_tile, 0)
    for t in range(tiles):
        for h in range(0, heads, 2):
            count = min(2, heads - h)
            both = [dqt[h + k, t] for k in range(count)]
            both = jnp.concatenate(both, axis=0) if count > 1 else both[0]
            out[t * tile : (t + 1) * tile, h * HD : (h + count) * HD] = (both.T * scale).astype(BF16)
    sums[...] = column_sum(out[...].astype(F32))


def attend_back(lengths, place, pieces, grads, mixed, lse, start, heads):
    own_rows = pieces[0].shape[0]
    width = heads * HD
    pairs = (heads + 1) // 2
    rows = own_rows * len(pieces)
    tile = min(256, rows)
    tiles = rows // tile
    body = functools.partial(attend_back_body, lengths.shape[0], start, heads, tile, len(pieces))
    return call(
        body,
        (1,),
        [scalars(), scalars()]
        + [whole(piece.shape) for piece in pieces]
        + [whole(grad.shape) for grad in grads]
        + [whole(mixed.shape), whole(lse.shape)],
        [whole((rows, 3 * width)), whole((1, 3 * width))],
        [like((rows, 3 * width), BF16), like((1, 3 * width), F32)],
        rows * rows * width * 5,
        16 * rows * width,
        [
            pltpu.VMEM((heads, tiles, tile, 2 * HD), BF16),
            pltpu.VMEM((heads, tiles, tile, 2 * HD), BF16),
            pltpu.VMEM((heads, tiles, tile, 2 * HD), BF16),
            pltpu.VMEM((heads, tiles, HD, tile), BF16),
            pltpu.VMEM((pairs, tiles, tile, 2 * HD), BF16),
            pltpu.VMEM((heads, tiles, tile, 2 * HD), BF16),
            pltpu.VMEM((heads, tiles, 1, tile), F32),
            pltpu.VMEM((heads, tile, 2 * HD), F32),
            pltpu.VMEM((heads, tile, 2 * HD), F32),
            pltpu.VMEM((heads, tiles, HD, tile), F32),
        ],
        limit=20,
    )(lengths, place, *pieces, *grads, mixed, lse)


def branch_body(item_count, piece_count, lengths, place, *refs):
    mixed = refs[:piece_count]
    weights = refs[piece_count : 2 * piece_count]
    stream0, shift, gain, bias, stream1, normed, squares = refs[2 * piece_count :]
    tile = stream0.shape[0]
    attn = shift[...]
    for left, right in zip(mixed, weights):
        attn = attn + mxu(left[...], right[...], NN)
    first = place[0] * (tile * pl.num_programs(0)) + pl.program_id(0) * tile
    valid = valid_column(lengths, item_count, first, tile)
    stream = stream0[...] + attn
    stream1[...] = stream
    scaled, _ = normalize(stream)
    normed[...] = (scaled * gain[...] + bias[...]).astype(BF16)

    @pl.when(pl.program_id(0) == 0)
    def _():
        squares[...] = jnp.zeros(squares.shape, F32)

    squares[...] += column_sum(valid * attn * attn)


def branch(lengths, place, mixed, weights, stream0, shift, gain, bias):
    rows, width = stream0.shape
    tile = min(256, rows)
    count = len(mixed)
    block = pl.BlockSpec((tile, width), lambda i: (i, 0))
    narrow = pl.BlockSpec((tile, mixed[0].shape[1]), lambda i: (i, 0))
    line = whole((1, width))
    return call(
        functools.partial(branch_body, lengths.shape[0], count),
        (rows // tile,),
        [scalars(), scalars()]
        + [narrow] * count
        + [whole(weights[0].shape)] * count
        + [block, line, line, line],
        [block, block, line],
        [like((rows, width), F32), like((rows, width), BF16), like((1, width), F32)],
        2 * rows * width * width,
        rows * width * 12 + 2 * width * width,
    )(lengths, place, *mixed, *weights, stream0, shift, gain, bias)


def feed_body(normed, grad_mlp, w_up, up_bias, w_down, act_out, upin_out, mlp_out, norm_out, bias_out):
    hidden = w_up.shape[1]
    chunk = min(512, hidden)
    left, grad = normed[...], grad_mlp[...]
    mlp = norm = None

    @pl.when(pl.program_id(0) == 0)
    def _():
        bias_out[...] = jnp.zeros(bias_out.shape, F32)

    for c in range(0, hidden, chunk):
        here = slice(c, c + chunk)
        up = mxu(left, w_up[:, here], NN) + up_bias[:, here]
        grad_act = mxu(grad, w_down[here, :], NT)
        size = jnp.abs(up)
        decay = jnp.exp(-0.5 * up * up)
        t = 1.0 / (1.0 + (0.3275911 * 0.7071067811865476) * size)
        series = t * (
            0.254829592
            + t * (-0.284496736 + t * (1.421413741 + t * (-1.453152027 + t * 1.061405429)))
        )
        tail = 0.5 * series * decay
        share = jnp.where(up >= 0.0, 1.0 - tail, tail)
        act = (up * share).astype(BF16)
        upin = ((share + up * decay * 0.3989422804014327) * grad_act).astype(BF16)
        act_out[:, here] = act
        upin_out[:, here] = upin
        bias_out[:, here] += column_sum(upin.astype(F32))
        mlp_part = mxu(act, w_down[here, :], NN)
        norm_part = mxu(upin, w_up[:, here], NT)
        mlp = mlp_part if mlp is None else mlp + mlp_part
        norm = norm_part if norm is None else norm + norm_part
    mlp_out[...] = mlp.astype(BF16)
    norm_out[...] = norm.astype(BF16)


def feed(normed, grad_mlp, w_up, up_bias, w_down):
    rows, width = normed.shape
    hidden = w_up.shape[1]
    tile = min(512, rows)
    block = pl.BlockSpec((tile, width), lambda i: (i, 0))
    wide = pl.BlockSpec((tile, hidden), lambda i: (i, 0))
    return call(
        feed_body,
        (rows // tile,),
        [block, block, whole(w_up.shape), whole((1, hidden)), whole(w_down.shape)],
        [wide, wide, block, block, whole((1, hidden))],
        [
            like((rows, hidden), BF16),
            like((rows, hidden), BF16),
            like((rows, width), BF16),
            like((rows, width), BF16),
            like((1, hidden), F32),
        ],
        8 * rows * width * hidden,
        12 * rows * width + 4 * width * hidden,
        limit=24,
    )(normed, grad_mlp, w_up, up_bias, w_down)


def splits(rows, bits):
    return bits and rows % (16 * 2 ** len(bits)) == 0


def position(ordinal, here, bits):
    number = sum(bit for k, bit in enumerate(bits) if ordinal >> k & 1)
    found, step = 0, 2 ** len(bits) // 2
    for bit in bits:
        found = found + jnp.where((number ^ here) & bit != 0, step, 0)
        step //= 2
    return found


def put(value, first_row, bits, here, kept, sent):
    if sent is None:
        kept[first_row : first_row + value.shape[0]] = value
        return
    half = kept.shape[0]
    size = 2 * half // 2 ** len(bits)
    step = math.gcd(size, value.shape[0])
    for row in range(first_row, first_row + value.shape[0], step):
        spot = position(row // size, here, bits) * size + row % size
        part = value[row - first_row : row - first_row + step]

        @pl.when(spot < half)
        def _():
            kept[pl.ds(pl.multiple_of(spot, 16), step)] = part

        @pl.when(spot >= half)
        def _():
            sent[pl.ds(pl.multiple_of(spot - half, 16), step)] = part


def outer_body(groups, tile, count, based, place, *refs):
    pairs = sum(len(halves) for _, _, halves in groups)
    base, refs = refs[:based], refs[based:]
    left, right, outs = refs[: -count - pairs], refs[-count - pairs : -pairs], list(refs[-pairs:])
    for start, bits, halves in groups:
        kept = outs.pop(0)
        sent = outs.pop(0) if len(halves) > 1 else None
        rows = sum(halves)
        step = tile if rows % tile == 0 else rows
        for first in range(0, rows, step):
            total = base[0][start + first : start + first + step] if base else None
            for p in range(count):
                if len(left) == count:
                    a = left[p][:, start + first : start + first + step]
                else:
                    size = right[0].shape[0]
                    a = left[0][p * size : (p + 1) * size, start + first : start + first + step]
                term = mxu(a, right[p][...], TN)
                total = term if total is None else total + term
            put(total.astype(kept.dtype), first, bits, place[1], kept, sent)


def outer(place, left, right, groups, base=(), dtype=BF16):
    rows, width = right[0].shape
    count = len(right)
    found, start = [], 0
    for size, bits in groups:
        halves = [size // 2] * 2 if splits(size, bits) else [size]
        found.append((start, bits, halves))
        start += size
    outs = [rows_out for _, _, halves in found for rows_out in halves]
    results = call(
        functools.partial(outer_body, found, 256, count, len(base)),
        (1,),
        [scalars()] + [whole(a.shape) for a in (*base, *left)] + [whole((rows, width))] * count,
        [whole((rows_out, width)) for rows_out in outs],
        [like((rows_out, width), dtype) for rows_out in outs],
        0,
        0,
        limit=24,
    )(place, *base, *left, *right)
    results = list(results)
    return [[results.pop(0) for _ in halves] for _, _, halves in found]


def each_body(bits, count, place, *refs):
    for left, out in zip(refs[:count], refs[count + 1 :]):
        value = mxu(left[...], refs[count][...], TN).astype(BF16)
        depth = value.shape[0]
        if splits(depth, bits):
            put(value, 0, bits, place[1], out.at[: depth // 2], out.at[depth // 2 :])
        else:
            out[...] = value


def outer_each(place, left, right, bits):
    rows, depth = left[0].shape
    width = right.shape[1]
    count = len(left)
    return call(
        functools.partial(each_body, bits, count),
        (1,),
        [scalars()] + [whole((rows, depth))] * count + [whole((rows, width))],
        [whole((depth, width))] * count,
        [like((depth, width), BF16)] * count,
        2 * count * rows * depth * width,
        2 * (count * rows * depth + rows * width + count * depth * width),
    )(place, *left, right)


def unpack_body(bits, sections, place, first, second, *outs):
    half, shares = first.shape[0], 2 ** len(bits)
    size = 2 * half // shares
    for block in range(shares):
        spot = position(block, place[1], bits) * size
        offset = 0
        for out, rows in zip(outs, sections):
            count = rows // shares
            start = spot + offset
            low = pl.ds(pl.multiple_of(jnp.minimum(start, half - count), 16), count)
            high = pl.ds(pl.multiple_of(jnp.maximum(start - half, 0), 16), count)
            part = jnp.where(spot < half, first[low], second[high])
            out[block * count : (block + 1) * count] = part.astype(out.dtype)
            offset += count


def unpack(place, first, second, bits, sections, dtype=F32):
    half, width = first.shape
    return call(
        functools.partial(unpack_body, bits, sections),
        (1,),
        [scalars(), whole(first.shape), whole(second.shape)],
        [whole((rows, width)) for rows in sections],
        [like((rows, width), dtype) for rows in sections],
        2 * half * width,
        12 * half * width,
    )(place, first, second)


def project_body(group_count, piece_count, *refs):
    grads = refs[:group_count]
    weights = refs[group_count : 2 * group_count]
    normed = refs[2 * group_count : 2 * group_count + piece_count]
    outs = refs[2 * group_count + piece_count : -1]
    sums = refs[-1]
    size = normed[0].shape[0]
    plain = weighed = 0.0
    for p in range(piece_count):
        total = None
        for grad, weight in zip(grads, weights):
            term = mxu(grad[p * size : (p + 1) * size], weight[...], NN)
            total = term if total is None else total + term
        outs[p][...] = total.astype(BF16)
        plain = plain + column_sum(total)
        weighed = weighed + column_sum(total * normed[p][...].astype(F32))
    sums[0:1] = plain
    sums[1:2] = weighed


def project_back(grads, weights, normed):
    size, width = normed[0].shape
    depth = sum(w.shape[0] for w in weights)
    count = len(normed)
    results = call(
        functools.partial(project_body, len(grads), count),
        (1,),
        [whole(g.shape) for g in grads] + [whole(w.shape) for w in weights] + [whole((size, width))] * count,
        [whole((size, width))] * count + [whole((8, width))],
        [like((size, width), BF16)] * count + [like((8, width), F32)],
        2 * count * size * depth * width,
        2 * count * size * (depth + 2 * width) + 2 * depth * width,
        limit=20,
    )(*grads, *weights, *normed)
    return list(results[:-1]), results[-1][:2]


def second_back_body(item_count, piece_count, lengths, place, half_a, half_b, stream1, cotangent, gain, *refs):
    weights = refs[:piece_count]
    grad_out, attn_out = refs[piece_count : piece_count + 2]
    mixed_out = refs[piece_count + 2 : 2 * piece_count + 2]
    sums = refs[-1]
    tile = stream1.shape[0]
    first = place[0] * (tile * pl.num_programs(0)) + pl.program_id(0) * tile
    valid = valid_column(lengths, item_count, first, tile)
    grad_norm = half_a[...].astype(F32) + half_b[...].astype(F32)
    scaled, rstd = normalize(stream1[...])
    grad = valid * cotangent[...].astype(F32) + norm_back(grad_norm, scaled, gain[...], rstd)
    grad_out[...] = grad
    rounded = grad.astype(BF16)
    attn_out[...] = rounded

    @pl.when(pl.program_id(0) == 0)
    def _():
        sums[...] = jnp.zeros(sums.shape, F32)

    sums[0:1] += column_sum(grad_norm * scaled)
    sums[1:2] += column_sum(grad_norm)
    sums[2:3] += column_sum(rounded.astype(F32))
    for weight, mixed in zip(weights, mixed_out):
        mixed[...] = mxu(rounded, weight[...], NT).astype(BF16)


def second_back(lengths, place, half_a, half_b, stream1, cotangent, gain, weights):
    rows, width = stream1.shape
    tile = min(256, rows)
    count = len(weights)
    depth = weights[0].shape[0]
    block = pl.BlockSpec((tile, width), lambda i: (i, 0))
    narrow = pl.BlockSpec((tile, depth), lambda i: (i, 0))
    results = call(
        functools.partial(second_back_body, lengths.shape[0], count),
        (rows // tile,),
        [scalars(), scalars(), block, block, block, block, whole((1, width))]
        + [whole(weights[0].shape)] * count,
        [block, block] + [narrow] * count + [whole((8, width))],
        [like((rows, width), F32), like((rows, width), BF16)]
        + [like((rows, depth), BF16)] * count
        + [like((8, width), F32)],
        2 * rows * width * width,
        rows * width * 20 + 2 * width * width,
    )(lengths, place, half_a, half_b, stream1, cotangent, gain, *weights)
    return results[0], results[1], results[2:-1], results[-1][:3]


def output_body(item_count, lengths, place, half_a, half_b, shift, stream1, cotangent, out, sums):
    tile = stream1.shape[0]
    first = place[0] * (tile * pl.num_programs(0)) + pl.program_id(0) * tile
    valid = valid_column(lengths, item_count, first, tile)
    mlp = half_a[...].astype(F32) + half_b[...].astype(F32) + shift[...]
    stream2 = stream1[...] + mlp
    out[...] = (valid * stream2).astype(BF16)

    @pl.when(pl.program_id(0) == 0)
    def _():
        sums[...] = jnp.zeros(sums.shape, F32)

    sums[0:1] += column_sum(valid * stream2 * stream2)
    sums[1:2] += column_sum(valid * mlp * mlp)
    sums[2:3] += column_sum((valid * cotangent[...].astype(F32)).astype(BF16).astype(F32))
    sums[3:4] += jnp.broadcast_to(column_sum(valid), (1, stream1.shape[1]))


def output_end(lengths, place, half_a, half_b, shift, stream1, cotangent):
    rows, width = stream1.shape
    tile = min(256, rows)
    block = pl.BlockSpec((tile, width), lambda i: (i, 0))
    out, sums = call(
        functools.partial(output_body, lengths.shape[0]),
        (rows // tile,),
        [scalars(), scalars(), block, block, whole((1, width)), block, block],
        [block, whole((8, width))],
        [like((rows, width), BF16), like((8, width), F32)],
        12 * rows * width,
        rows * width * 12,
    )(lengths, place, half_a, half_b, shift, stream1, cotangent)
    return out, sums[:4]


def input_body(half_a, half_b, stream0, grad_stream1, gain, out):
    grad_norm = half_a[...].astype(F32) + half_b[...].astype(F32)
    scaled, rstd = normalize(stream0[...])
    out[...] = grad_stream1[...] + norm_back(grad_norm, scaled, gain[...].astype(F32), rstd)


def input_end(half_a, half_b, stream0, grad_stream1, gain):
    rows, width = stream0.shape
    tile = min(256, rows)
    block = pl.BlockSpec((tile, width), lambda i: (i, 0))
    return call(
        input_body,
        (rows // tile,),
        [block, block, block, block, whole((1, width))],
        block,
        like((rows, width), F32),
        12 * rows * width,
        rows * width * 16,
    )(half_a, half_b, stream0, grad_stream1, gain)


def swap(array, axis, bit):
    return lax.ppermute(array, axis, [(i, i ^ bit) for i in range(lax.axis_size(axis))])


def after(array, *others):
    return lax.optimization_barrier((array, *others))[0]


def spread(own, top):
    pieces, bit = {0: own}, top // 2
    while bit:
        for p in sorted(pieces):
            pieces[p | bit] = swap(pieces[p], "mp", bit)
        bit //= 2
    return [pieces[p] for p in range(len(pieces))]


def add(left, right):
    return (left.astype(F32) + right.astype(F32)).astype(left.dtype)


def fold(parts, *others):
    bit = 1
    while len(parts) > 1:
        came = [swap(parts[p + 1], "mp", bit) for p in range(0, len(parts), 2)]
        if others:
            came = [after(array, *others) for array in came]
        parts = [add(parts[2 * k], array) for k, array in enumerate(came)]
        bit *= 2
    return parts[0]


def exchange(parts):
    return [parts[0]] + [swap(parts[p], "mp", p) for p in range(1, len(parts))]


def total(array, axis):
    bit = 1
    while bit < lax.axis_size(axis):
        array = array + swap(array, axis, bit)
        bit *= 2
    return array


def own_block(place, weight, bits):
    if not splits(weight.shape[0], bits):
        return weight
    size = weight.shape[0] // 2 ** len(bits)
    return lax.dynamic_slice_in_dim(weight, place[1] * size, size, 0)


def join_blocks(place, kept, rows, bits):
    if kept.shape[0] == rows:
        return kept
    for bit in bits[:0:-1]:
        kept = jnp.concatenate([kept, swap(kept, "dp", bit)], axis=0)
    return unpack(place, kept, swap(kept, "dp", bits[0]), bits, [rows], kept.dtype)[0]


class DpSum:
    def __init__(self, place, parts, bits, *others):
        self.place, self.bits, self.steps = place, bits, 0
        self.sections = [sum(half.shape[0] for half in halves) for halves in parts]
        blocks, width = max(2 ** (len(bits) - 1) // 2, 1), parts[0][0].shape[1]
        halves = [
            jnp.concatenate([half.reshape(blocks, -1, width) for half in group], axis=1).reshape(-1, width)
            for group in zip(*parts)
        ]
        if len(halves) == 1:
            self.kept = lax.psum(halves[0], "dp")
            return
        self.kept, self.sent = halves
        self.came = swap(after(self.sent, *others), "dp", bits[0])

    def step(self, *others):
        if not self.more():
            return
        self.steps += 1
        came, count = after(self.came, *others), len(self.bits)
        if self.steps < count:
            half = came.shape[0] // 2
            self.sent = add(self.kept[half:], came[half:])
            self.kept = add(self.kept[:half], came[:half])
            if self.steps == count - 1:
                self.kept = self.sent = jnp.concatenate([self.kept, self.sent], axis=0)
            self.came = swap(self.sent, "dp", self.bits[self.steps])
        else:
            if self.steps == count:
                self.kept = add(self.kept, came)
            else:
                self.kept = jnp.concatenate([self.kept, came], axis=0)
            self.sent = self.kept
            self.came = swap(self.kept, "dp", self.bits[2 * count - 2 - self.steps])

    def now(self):
        return [self.kept, self.sent] if hasattr(self, "came") else []

    def more(self):
        return hasattr(self, "came") and self.steps < 2 * len(self.bits) - 2

    def done(self, *others):
        if not hasattr(self, "came"):
            return [self.kept.astype(F32)]
        came = after(self.came, *others) if others else self.came
        return unpack(self.place, self.kept, came, self.bits[:-1], self.sections)


def advance(chains, others):
    for chain in chains:
        chain.step(*others)
    return [array for chain in chains for array in chain.now()] or list(others)


def per_device(
    tokens, cotangent, lengths, gsd_ratio, ln1_gain, ln1_bias, w_qkv, qv_bias, w_out, out_bias,
    ln2_gain, ln2_bias, w_up, up_bias, w_down, down_bias,
):
    own_rows, width = tokens.shape
    mp_count, dp_count = lax.axis_size("mp"), lax.axis_size("dp")
    top = mp_count // 2
    low_first = [1 << k for k in range(dp_count.bit_length() - 1)] if dp_count & (dp_count - 1) == 0 else []
    low_second = low_first[1:2] + low_first[:1] + low_first[2:]
    low_last = low_first[1:] + low_first[:1]
    place = jnp.stack([lax.axis_index("mp"), lax.axis_index("dp")]).astype(jnp.int32)
    depth = w_qkv.shape[1]
    heads = depth // HD
    gain2, bias2 = ln2_gain[None], ln2_bias[None]
    up_shift = up_bias[None]

    w_out_block = swap(own_block(place, w_out, low_first), "mp", top)
    grad_mlp_own = mask_rows(lengths, place, cotangent)
    early = own_rows // 8
    grad_mlp_far = swap(grad_mlp_own[:early], "mp", top)
    tokens = after(tokens, w_out_block)
    stream0, normed1_own = encode(lengths, gsd_ratio, place, tokens, ln1_gain[None], ln1_bias[None])
    normed1_far = swap(after(normed1_own, grad_mlp_far), "mp", top)
    w_out_far = join_blocks(place, w_out_block, depth, low_first)
    normed1 = spread(normed1_own, top)
    w_flat = w_qkv.reshape(3 * depth, width)
    shift = jnp.concatenate([qv_bias[0], jnp.zeros((depth,), F32), qv_bias[1]])[None]

    def project(piece):
        return (mxu(piece, w_flat, NT) + shift).astype(BF16)

    qkv = [project(piece) for piece in normed1]
    grad_mlp = spread(grad_mlp_own, top)
    w_out_all = spread(w_out, top)
    normed1_far = after(normed1_far, w_out_far, *qkv, *grad_mlp, *w_out_all)
    grad_mlp_late = swap(after(grad_mlp_own[early:], normed1_far), "mp", top)
    normed1 += spread(normed1_far, top)
    w_out_all += spread(w_out_far, top)
    qkv += [project(piece) for piece in normed1[top:]]

    attended, logsum = attend(lengths, place, qkv)
    attended, grad_mlp_late = lax.optimization_barrier((attended, grad_mlp_late))
    grad_mlp_far = jnp.concatenate([grad_mlp_far, grad_mlp_late], axis=0)
    mixed = exchange([attended[p * own_rows : (p + 1) * own_rows] for p in range(mp_count)])
    grad_mlp += spread(grad_mlp_far, top)
    mixed[0] = after(mixed[0], *grad_mlp)
    stream1, normed2_own, attn_squares = branch(
        lengths, place, mixed, w_out_all, stream0, out_bias[None], gain2, bias2
    )

    normed2_far = swap(normed2_own, "mp", top)
    normed2 = spread(normed2_own, top)
    fed = [feed(normed2[p], grad_mlp[p], w_up, up_shift, w_down) for p in range(top)]
    [[down_base]] = outer(place, [f[0] for f in fed], grad_mlp[:top], [(w_down.shape[0], [])], dtype=F32)
    [[up_base]] = outer(place, normed2, [f[1] for f in fed], [(width, [])], dtype=F32)
    far_normed = spread(after(normed2_far, down_base, up_base), top)
    norm2_near, mlp_near = fold([f[3] for f in fed]), fold([f[2] for f in fed])
    far_normed[-1] = after(far_normed[-1], norm2_near, mlp_near)
    right = grad_mlp[top:]
    far_fed = [feed(n, g, w_up, up_shift, w_down) for n, g in zip(far_normed, right)]
    norm2_part = fold([f[3] for f in far_fed])
    norm2_far = swap(norm2_part, "mp", top)
    acts, upins = [f[0] for f in far_fed], [f[1] for f in far_fed]
    acts[-1] = after(acts[-1], norm2_part)
    [down_halves] = outer(place, acts, right, [(w_down.shape[0], low_first[:-1])], [down_base])
    grad_down = DpSum(place, [down_halves], low_first)
    upins[-1] = after(upins[-1], *down_halves)
    [up_halves] = outer(place, far_normed, upins, [(width, low_last[:-1])], [up_base])
    grad_up = DpSum(place, [up_halves], low_last)
    grad_up_bias = functools.reduce(jnp.add, [f[4] for f in fed + far_fed])
    norm2_far = after(norm2_far, *up_halves)
    grad_stream1, grad_attn, grad_mixed, second_sums = second_back(
        lengths, place, norm2_near, norm2_far, stream1, cotangent, gain2, w_out_all
    )

    grads = exchange(list(grad_mixed))
    out_parts = outer_each(place, mixed, grad_attn, low_first[:-1])
    out_near, out_part = fold(out_parts[:top]), fold(out_parts[top:])
    mlp_part = fold([f[2] for f in far_fed])
    now = advance([grad_down, grad_up], grads)
    grads[-1] = after(grads[-1], out_near, out_part, mlp_part, *now)
    out_far = swap(after(out_part, grads[-1]), "mp", top)
    mlp_far = swap(after(mlp_part, grads[-1]), "mp", top)
    proj, proj_sums = attend_back(lengths, place, qkv, grads, attended, logsum, 0, heads)
    now = advance([grad_down, grad_up], [proj])
    qkv_rows = 3 * depth // 2
    halves_a, halves_b = outer(
        place, [after(proj, *now)], normed1, [(qkv_rows, low_first[:-1]), (qkv_rows, low_second[:-1])]
    )
    out_far = after(out_far, *halves_a)
    out_sum = add(out_near, out_far)
    groups_a = [halves_a]
    if len(halves_a) > 1 and splits(depth, low_first[:-1]):
        groups_a.append([out_sum[: depth // 2], out_sum[depth // 2 :]])
    grad_a, grad_b = DpSum(place, groups_a, low_first), DpSum(place, [halves_b], low_second)
    main, proj_chains = [grad_down, grad_up], [grad_a, grad_b]
    now = [*now, *grad_a.now(), *grad_b.now()]
    parts, first_sums = project_back([after(proj, *now)], [w_flat], normed1)
    chains = main + proj_chains
    mp_hops = [1 << k for k in range(mp_count.bit_length() - 1)]
    dp_hops = [low_first[0], *low_first[:0:-1]] if low_first else []

    def hop(array, axis, hops, *others):
        return array + after(swap(array, axis, hops.pop(0)), *others) if hops else array

    norm1_part, norm1_near = fold(parts[top:], first_sums), fold(parts[:top], first_sums)
    now = advance(chains, [first_sums])

    norm1_far = swap(norm1_part, "mp", top)
    output, output_sums = output_end(
        lengths, place, after(mlp_near, *now), mlp_far, down_bias[None], stream1, cotangent
    )
    rows = jnp.concatenate([first_sums, second_sums, output_sums, attn_squares], axis=0)
    while len(mp_hops) > 1:
        rows = hop(rows, "mp", mp_hops, output_sums)
    flat = jnp.concatenate([grad_up_bias[0], proj_sums[0, :depth], proj_sums[0, 2 * depth :]])
    flat = jnp.pad(flat, (0, -flat.size % 1024)).reshape(-1, 128)
    flat = jnp.concatenate([rows.reshape(-1, 128), flat], axis=0)
    flat = hop(flat, "dp", dp_hops, norm1_near)
    norm1_far = after(norm1_far, flat)
    now = advance(chains, [flat])

    input_grad = input_end(
        norm1_near, norm1_far, after(stream0, *now), grad_stream1, ln1_gain[None]
    )
    flat = jnp.concatenate(
        [hop(flat[: rows.size // 128], "mp", mp_hops, input_grad), flat[rows.size // 128 :]], axis=0
    )
    now = advance(proj_chains, [input_grad, flat])
    while any(chain.more() for chain in main):
        now = advance(main, now)

    [grad_down], [grad_up] = grad_down.done(*now), grad_up.done(*now)
    while dp_hops or any(chain.more() for chain in proj_chains):
        flat = hop(flat, "dp", dp_hops, grad_down, grad_up)
        now = advance(proj_chains, [grad_down, grad_up, flat])

    grad_a, grad_b = grad_a.done(), grad_b.done()
    grad_out_weight = grad_a[1] if len(grad_a) > 1 else lax.psum(out_sum, "dp").astype(F32)
    grad_qkv = jnp.concatenate([grad_a[0], grad_b[0]], axis=0).reshape(3, depth, width)
    flat = flat.reshape(-1)
    rows = flat[: rows.size].reshape(rows.shape)
    up_sums = flat[rows.size : rows.size + up_bias.shape[0]]
    proj_sums = flat[rows.size + up_bias.shape[0] :][: 2 * depth].reshape(2, depth)
    squares = jnp.stack([jnp.sum(rows[5]), jnp.sum(rows[9]), jnp.sum(rows[6])])
    stats = jnp.sqrt(squares / (rows[8, 0] * width))
    grad_ln1_gain = (rows[1] - ln1_bias.astype(F32) * rows[0]) / ln1_gain.astype(F32)
    return (
        output, input_grad, grad_ln1_gain, rows[0], grad_qkv, proj_sums, grad_out_weight, rows[4],
        rows[2], rows[3], grad_up, up_sums, grad_down, rows[7], stats,
    )


def solution(mesh):
    rows, one = P(("dp", "mp"), None), P()
    placed = (
        rows, rows, P("dp"), P("dp"), one, one, P(None, "mp", None), P(None, "mp"), P("mp", None), one,
        one, one, P(None, "mp"), P("mp"), P("mp", None), one,
    )
    results = (
        rows, rows, one, one, P(None, "mp", None), P(None, "mp"), P("mp", None), one,
        one, one, P(None, "mp"), P("mp"), P("mp", None), one, one,
    )
    return jax.shard_map(per_device, mesh=mesh, in_specs=placed, out_specs=results, check_vma=False)
```

profile of v0, /device:TPU:0, one launch (start us, length us, event | category | flops | bytes accessed | tf_op | source)
XLA Modules:
  0.0 337.4 jit_solution(7666597766683967146)
XLA Ops:
  2.1 2.5 collective-permute-start
  9.2 3.3 shard_map.280
  12.7 2.9 collective-permute-start.4
  17.1 2.5 collective-permute-done.4
  20.5 4.2 %collective-permute-done.5 = bf16[64,1024]{1,0:T(8,128)(2,1)S(1)} collective-permute-done((bf16[64,1024]{1,0:T(8,128)(2,1)S(1)}, bf16[64,1024]{1,0:T(8,128)(2,1)S(1)}, u32[]{:S(2)}, u32[]{:S(2)}) %collective-permute-start.5) | collective-permute-done | bytes 131104 | tf_op jit(solution)/shard_map/ppermute | solution.py:833
  27.4 3.8 %collective-permute-done.6.second = bf16[128,1024]{1,0:T(8,128)(2,1)S(1)} collective-permute-done((bf16[128,1024]{1,0:T(8,128)(2,1)S(1)}, bf16[128,1024]{1,0:T(8,128)(2,1)S(1)}, u32[]{:S(2)}, u32[]{:S(2)}) %collective-permute-start.6) | collective-permute-done | bytes 262176 | tf_op jit(solution)/shard_map/ppermute | solution.py:833
  32.9 8.0 %collective-permute-done.3.refs_3_.refs_4_ = bf16[512,1024]{1,0:T(8,128)(2,1)S(1)} collective-permute-done((bf16[512,1024]{1,0:T(8,128)(2,1)S(1)}, bf16[512,1024]{1,0:T(8,128)(2,1)S(1)}, u32[]{:S(2)}, u32[]{:S(2)}) %collective-permute-start.3) | collective-permute-done | bytes 1048608 | tf_op jit(solution)/shard_map/ppermute | solution.py:833
  44.6 17.2 %shard_map.283 = (bf16[2048,256]{1,0:T(8,128)(2,1)S(1)}, f32[4,8,1,256]{3,2,1,0:T(1,128)S(1)}) custom-call(s32[5]{0:T(128)S(1)} %copy-done.21, s32[2]{0:T(128)S(1)} %pad_add_fusion.place.place_ref, bf16[512,768]{1,0:T(8,128)(2,1)S(1)} %add_convert_fusion.9.refs_0_, bf16[512,768]{1,0:T(8,128)(2,1)S(1)} %add_convert_fusion.8.refs_1_, ...), custom_call_target="tpu_custom_call" | custom-call | tf_op jit(solution)/shard_map/pallas_call | solution.py:317
  61.8 1.9 collective-permute-done.10
  67.3 5.6 %collective-permute-done.14.refs_3_ = bf16[512,256]{1,0:T(8,128)(2,1)S(1)} collective-permute-done((bf16[512,256]{1,0:T(8,128)(2,1)S(1)}, bf16[512,256]{1,0:T(8,128)(2,1)S(1)}, u32[]{:S(2)}, u32[]{:S(2)}) %collective-permute-start.14) | collective-permute-done | bytes 262176 | tf_op jit(solution)/shard_map/ppermute | solution.py:833
  72.9 5.9 %collective-permute-done.13.refs_2_ = bf16[512,256]{1,0:T(8,128)(2,1)S(1)} collective-permute-done((bf16[512,256]{1,0:T(8,128)(2,1)S(1)}, bf16[512,256]{1,0:T(8,128)(2,1)S(1)}, u32[]{:S(2)}, u32[]{:S(2)}) %collective-permute-start.13) | collective-permute-done | bytes 262176 | tf_op jit(solution)/shard_map/ppermute | solution.py:833
  78.8 3.3 shard_map.284
  84.9 6.4 %shard_map.286 = (bf16[512,1024]{1,0:T(8,128)(2,1)S(1)}, bf16[512,1024]{1,0:T(8,128)(2,1)S(1)}, bf16[512,1024]{1,0:T(8,128)(2,1)S(1)}, bf16[512,1024]{1,0:T(8,128)(2,1)}, f32[1,1024]{1,0:T(1,128)S(1)}) custom-call(bf16[512,1024]{1,0:T(8,128)(2,1)S(1)} %collective-permute-done.16.normed.refs_1_, ...), custom_call_target="tpu_custom_call" | custom-call | tf_op jit(solution)/shard_map/pallas_call | solution.py:542
  91.8 5.4 %shard_map.285 = (bf16[512,1024]{1,0:T(8,128)(2,1)S(1)}, bf16[512,1024]{1,0:T(8,128)(2,1)S(1)}, bf16[512,1024]{1,0:T(8,128)(2,1)S(1)}, bf16[512,1024]{1,0:T(8,128)(2,1)S(1)}, f32[1,1024]{1,0:T(1,128)S(1)}) custom-call(bf16[512,1024]{1,0:T(8,128)(2,1)S(1)} %get-tuple-element.128.normed.refs_0_, bf16[512,1024]{1,0:T(8,128)(2,1)S(1)} %shard_map.281.grad_mlp.refs_2_, ...), custom_call_target="tpu_custom_call" | custom-call | tf_op jit(solution)/shard_map/pallas_call | solution.py:542
  97.2 2.9 shard_map.287.refs_0_
  100.1 3.4 %shard_map.288.refs_0_ = f32[1024,1024]{1,0:T(8,128)S(1)} custom-call(s32[2]{0:T(128)S(1)} %pad_add_fusion.place.place_ref, bf16[512,1024]{1,0:T(8,128)(2,1)S(1)} %get-tuple-element.128.normed.refs_0_, bf16[512,1024]{1,0:T(8,128)(2,1)S(1)} %collective-permute-done.16.normed.refs_1_, bf16[512,1024]{1,0:T(8,128)(2,1)S(1)} %get-tuple-element.133.refs_2_, ...), custom_call_target="tpu_custom_call" | custom-call | tf_op jit(solution)/shard_map/pallas_call | solution.py:624
  103.5 4.4 %collective-permute-done.18.normed.refs_1_ = bf16[512,1024]{1,0:T(8,128)(2,1)S(1)} collective-permute-done((bf16[512,1024]{1,0:T(8,128)(2,1)S(1)}, bf16[512,1024]{1,0:T(8,128)(2,1)S(1)}, u32[]{:S(2)}, u32[]{:S(2)}) %collective-permute-start.18) | collective-permute-done | bytes 1048608 | tf_op jit(solution)/shard_map/ppermute | solution.py:833
  111.1 5.8 %shard_map.290 = (bf16[512,1024]{1,0:T(8,128)(2,1)S(1)}, bf16[512,1024]{1,0:T(8,128)(2,1)S(1)}, bf16[512,1024]{1,0:T(8,128)(2,1)}, bf16[512,1024]{1,0:T(8,128)(2,1)S(1)}, f32[1,1024]{1,0:T(1,128)S(1)}) custom-call(bf16[512,1024]{1,0:T(8,128)(2,1)S(1)} %collective-permute-done.19.normed.refs_2_, ...), custom_call_target="tpu_custom_call" | custom-call | tf_op jit(solution)/shard_map/pallas_call | solution.py:542
  117.4 5.4 %shard_map.289 = (bf16[512,1024]{1,0:T(8,128)(2,1)S(1)}, bf16[512,1024]{1,0:T(8,128)(2,1)S(1)}, bf16[512,1024]{1,0:T(8,128)(2,1)S(1)}, bf16[512,1024]{1,0:T(8,128)(2,1)S(1)}, f32[1,1024]{1,0:T(1,128)S(1)}) custom-call(bf16[512,1024]{1,0:T(8,128)(2,1)S(1)} %collective-permute-done.18.normed.refs_1_, ...), custom_call_target="tpu_custom_call" | custom-call | tf_op jit(solution)/shard_map/pallas_call | solution.py:542
  124.9 3.9 %shard_map.291 = (bf16[512,1024]{1,0:T(8,128)(2,1)S(1)}, bf16[512,1024]{1,0:T(8,128)(2,1)S(1)}) custom-call(s32[2]{0:T(128)S(1)} %pad_add_fusion.place.place_ref, f32[1024,1024]{1,0:T(8,128)S(1)} %shard_map.287.refs_0_, bf16[512,1024]{1,0:T(8,128)(2,1)S(1)} %get-tuple-element.136.refs_1_, bf16[512,1024]{1,0:T(8,128)(2,1)S(1)} %get-tuple-element.143.refs_2_, ...), custom_call_target="tpu_custom_call" | custom-call | tf_op jit(solution)/shard_map/pallas_call | solution.py:624
  128.8 3.7 %shard_map.292 = (bf16[512,1024]{1,0:T(8,128)(2,1)S(1)}, bf16[512,1024]{1,0:T(8,128)(2,1)S(1)}) custom-call(s32[2]{0:T(128)S(1)} %pad_add_fusion.place.place_ref, f32[1024,1024]{1,0:T(8,128)S(1)} %shard_map.288.refs_0_, bf16[512,1024]{1,0:T(8,128)(2,1)S(1)} %collective-permute-done.18.normed.refs_1_, ...), custom_call_target="tpu_custom_call" | custom-call | tf_op jit(solution)/shard_map/pallas_call | solution.py:624
  135.7 13.2 %collective-permute-done.23.half_b = bf16[512,1024]{1,0:T(8,128)(2,1)S(1)} collective-permute-done((bf16[512,1024]{1,0:T(8,128)(2,1)S(1)}, bf16[512,1024]{1,0:T(8,128)(2,1)S(1)}, u32[]{:S(2)}, u32[]{:S(2)}) %collective-permute-start.23) | collective-permute-done | bytes 1048608 | tf_op jit(solution)/shard_map/ppermute | solution.py:833
  149.0 4.3 %shard_map.293 = (f32[512,1024]{1,0:T(8,128)S(1)}, bf16[512,1024]{1,0:T(8,128)(2,1)S(1)}, bf16[512,256]{1,0:T(8,128)(2,1)S(1)}, bf16[512,256]{1,0:T(8,128)(2,1)S...) custom-call(s32[5]{0:T(128)S(1)} %copy-done.21, ...), custom_call_target="tpu_custom_call" | custom-call | tf_op jit(solution)/shard_map/pallas_call | solution.py:762
  156.1 2.9 shard_map.294
  160.5 3.2 collective-permute-done.25.refs_6_
  163.7 4.8 %collective-permute-done.26.refs_7_ = bf16[512,256]{1,0:T(8,128)(2,1)S(1)} collective-permute-done((bf16[512,256]{1,0:T(8,128)(2,1)S(1)}, bf16[512,256]{1,0:T(8,128)(2,1)S(1)}, u32[]{:S(2)}, u32[]{:S(2)}) %collective-permute-start.26) | collective-permute-done | bytes 262176 | tf_op jit(solution)/shard_map/ppermute | solution.py:833
  174.0 23.7 %shard_map.295 = (bf16[2048,768]{1,0:T(8,128)(2,1)S(1)}, f32[1,768]{1,0:T(1,128)S(1)}) custom-call(s32[5]{0:T(128)S(1)} %copy-done.21, s32[2]{0:T(128)S(1)} %pad_add_fusion.place.place_ref, bf16[512,768]{1,0:T(8,128)(2,1)S(1)} %add_convert_fusion.9.refs_0_, bf16[512,768]{1,0:T(8,128)(2,1)S(1)} %add_convert_fusion.8.refs_1_, ...), custom_call_target="tpu_custom_call" | custom-call | tf_op jit(solution)/shard_map/pallas_call | solution.py:430
  198.3 4.2 %collective-permute-start.32 = (bf16[256,1024]{1,0:T(8,128)(2,1)S(1)}, bf16[256,1024]{1,0:T(8,128)(2,1)S(1)}, u32[]{:S(2)}, u32[]{:S(2)}) collective-permute-start(bf16[256,1024]{1,0:T(8,128)(2,1)S(1)} %pad_maximum_fusion.5), channel_id=1, source_target_pairs={{0,16},{4,20},{8,24},{12,28},{16,0},{20,4},{24,8},{28,12},{1,17},{... | collective-permute-start | bytes 1572872 | tf_op jit(solution)/shard_map/ppermute | solution.py:833
  202.4 4.7 %shard_map.296 = (bf16[192,1024]{1,0:T(8,128)(2,1)S(1)}, bf16[192,1024]{1,0:T(8,128)(2,1)S(1)}, bf16[192,1024]{1,0:T(8,128)(2,1)S(1)}, bf16[192,1024]{1,0:T(8,128)(2,1)S(1)}) custom-call(s32[2]{0:T(128)S(1)} %pad_add_fusion.place.place_ref, bf16[2048,768]{1,0:T(8,128)(2,1)S(1)} %get-tuple-element.178.refs_0_, ...), custom_call_target="tpu_custom_call" | custom-call | tf_op jit(solution)/shard_map/pallas_call | solution.py:624
  208.5 4.7 %shard_map.297 = (bf16[512,1024]{1,0:T(8,128)(2,1)S(1)}, bf16[512,1024]{1,0:T(8,128)(2,1)}, bf16[512,1024]{1,0:T(8,128)(2,1)S(1)}, bf16[512,1024]{1,0:T(8,128)(2,1)}, f32[8,1024]{1,0:T(8,128)S(1)}) custom-call(bf16[2048,768]{1,0:T(8,128)(2,1)S(1)} %get-tuple-element.178.refs_0_, bf16[768,1024]{1,0:T(8,128)(2,1)S(1)} %bitcast.66, ...), custom_call_target="tpu_custom_call" | custom-call | tf_op jit(solution)/shard_map/pallas_call | solution.py:716
  213.3 14.6 %collective-permute-done.37 = bf16[192,1024]{1,0:T(8,128)(2,1)S(1)} collective-permute-done((bf16[192,1024]{1,0:T(8,128)(2,1)S(1)}, bf16[192,1024]{1,0:T(8,128)(2,1)S(1)}, u32[]{:S(2)}, u32[]{:S(2)}) %collective-permute-start.37) | collective-permute-done | bytes 393248 | tf_op jit(solution)/shard_map/ppermute | solution.py:833
  232.4 2.9 shard_map.298
  237.9 1.7 collective-permute-start.43
  239.7 1.9 add_convert_fusion.1.half_a
  245.5 22.7 %collective-permute-done.46 = bf16[160,1024]{1,0:T(8,128)(2,1)S(1)} collective-permute-done((bf16[160,1024]{1,0:T(8,128)(2,1)}, bf16[160,1024]{1,0:T(8,128)(2,1)S(1)}, u32[]{:S(2)}, u32[]{:S(2)}) %collective-permute-start.46) | collective-permute-done | bytes 327712 | tf_op jit(solution)/shard_map/ppermute | solution.py:833
  271.0 1.8 collective-permute-start.50
  275.7 3.0 collective-permute-start.51
  278.7 2.5 shard_map.299
  281.3 21.0 %collective-permute-done.52 = bf16[96,1024]{1,0:T(8,128)(2,1)S(1)} collective-permute-done((bf16[96,1024]{1,0:T(8,128)(2,1)S(1)}, bf16[96,1024]{1,0:T(8,128)(2,1)S(1)}, u32[]{:S(2)}, u32[]{:S(2)}) %collective-permute-start.52) | collective-permute-done | bytes 196640 | tf_op jit(solution)/shard_map/ppermute | solution.py:833
  302.3 7.0 %collective-permute-done.51 = bf16[160,1024]{1,0:T(8,128)(2,1)S(1)} collective-permute-done((bf16[160,1024]{1,0:T(8,128)(2,1)S(1)}, bf16[160,1024]{1,0:T(8,128)(2,1)S(1)}, u32[]{:S(2)}, u32[]{:S(2)}) %collective-permute-start.51) | collective-permute-done | bytes 327712 | tf_op jit(solution)/shard_map/ppermute | solution.py:833
  310.2 2.0 collective-permute-done.53.second
  312.1 2.8 shard_map.300
  315.0 2.8 shard_map.301
  319.5 3.4 %collective-permute-done.54 = f32[96,128]{1,0:T(8,128)S(1)} collective-permute-done((f32[96,128]{1,0:T(8,128)S(1)}, f32[96,128]{1,0:T(8,128)S(1)}, u32[]{:S(2)}, u32[]{:S(2)}) %collective-permute-start.54) | collective-permute-done | bytes 49184 | tf_op jit(solution)/shard_map/ppermute | solution.py:833
  326.7 2.5 fusion.8
  329.8 2.7 collective-permute-done.58.second
  333.3 1.7 shard_map.302
  334.9 2.0 pad_maximum_fusion
  (236 shorter events, 67.6 us)
Async XLA Ops:
  0.7 32.1 %collective-permute-start.8 = (bf16[256,1024]{1,0:T(8,128)(2,1)}, bf16[256,1024]{1,0:T(8,128)(2,1)S(1)}, u32[]{:S(2)}, u32[]{:S(2)}) collective-permute-start(bf16[256,1024]{1,0:T(8,128)(2,1)} %refs_0_.1), channel_id=1, source_target_pairs={{0,1},{1,0},{2,3},{3,2},{4,5},{5,4},{6,7},{7,6},{8,9},{9,8},{10,11... | collective-permute-start | bytes 1572872 | tf_op jit(solution)/shard_map/ppermute | solution.py:833
  7.3 25.6 %collective-permute-start.7 = (bf16[512,1024]{1,0:T(8,128)(2,1)S(1)}, bf16[512,1024]{1,0:T(8,128)(2,1)S(1)}, u32[]{:S(2)}, u32[]{:S(2)}) collective-permute-start(bf16[512,1024]{1,0:T(8,128)(2,1)S(1)} %shard_map.281.grad_mlp.refs_2_), channel_id=1, source_target_pairs={{0,1},{1,0},{2,3},{3,2},{4,5},{5,4},{6,7},{7,6},{8,9},{9,8},{10,11... | collective-permute-start | bytes 3145736 | tf_op jit(solution)/shard_map/ppermute | solution.py:833
  7.6 8.0 %collective-permute-start.2 = (bf16[64,1024]{1,0:T(8,128)(2,1)S(1)}, bf16[64,1024]{1,0:T(8,128)(2,1)S(1)}, u32[]{:S(2)}, u32[]{:S(2)}) collective-permute-start(bf16[64,1024]{1,0:T(8,128)(2,1)S(1)} %slice.278), channel_id=1, source_target_pairs={{0,2},{1,3},{2,0},{3,1},{4,6},{5,7},{6,4},{7,5},{8,10},{9,11},{10,... | collective-permute-start | bytes 393224 | tf_op jit(solution)/shard_map/ppermute | solution.py:833
  12.5 19.3 %collective-permute-start.1 = (bf16[512,1024]{1,0:T(8,128)(2,1)S(1)}, bf16[512,1024]{1,0:T(8,128)(2,1)S(1)}, u32[]{:S(2)}, u32[]{:S(2)}) collective-permute-start(bf16[512,1024]{1,0:T(8,128)(2,1)S(1)} %get-tuple-element.120.refs_1_.refs_2_), channel_id=1, source_target_pairs={{0,1},{1,0},{2,3},{3,2},{4,5},{5,4},{6,7},{7,6},{8,9},{9,8},{10,11... | collective-permute-start | bytes 3145736 | tf_op jit(solution)/shard_map/ppermute | solution.py:833
  12.7 7.0 %collective-permute-start.4 = (bf16[32,1024]{1,0:T(8,128)(2,1)S(1)}, bf16[32,1024]{1,0:T(8,128)(2,1)S(1)}, u32[]{:S(2)}, u32[]{:S(2)}) collective-permute-start(bf16[32,1024]{1,0:T(8,128)(2,1)S(1)} %collective-permute-done), channel_id=1, source_target_pairs={{0,16},{4,20},{8,24},{12,28},{16,0},{20,4},{24,8},{28,12},{1,17},{... | collective-permute-start | bytes 196616 | tf_op jit(solution)/shard_map/ppermute | solution.py:833
  15.6 25.3 %collective-permute-start.3 = (bf16[512,1024]{1,0:T(8,128)(2,1)S(1)}, bf16[512,1024]{1,0:T(8,128)(2,1)S(1)}, u32[]{:S(2)}, u32[]{:S(2)}) collective-permute-start(bf16[512,1024]{1,0:T(8,128)(2,1)S(1)} %get-tuple-element.120.refs_1_.refs_2_), channel_id=1, source_target_pairs={{0,2},{1,3},{2,0},{3,1},{4,6},{5,7},{6,4},{7,5},{8,10},{9,11},{10,... | collective-permute-start | bytes 3145736 | tf_op jit(solution)/shard_map/ppermute | solution.py:833
  24.7 6.5 %collective-permute-start.6 = (bf16[128,1024]{1,0:T(8,128)(2,1)S(1)}, bf16[128,1024]{1,0:T(8,128)(2,1)S(1)}, u32[]{:S(2)}, u32[]{:S(2)}) collective-permute-start(bf16[128,1024]{1,0:T(8,128)(2,1)S(1)} %constant_dynamic-update-slice_fusion.first), channel_id=1, source_target_pairs={{0,4},{4,0},{8,12},{12,8},{16,20},{20,16},{24,28},{28,24},{1,5},{5... | collective-permute-start | bytes 786440 | tf_op jit(solution)/shard_map/ppermute | solution.py:833
  40.9 22.8 %collective-permute-start.10 = (bf16[448,1024]{1,0:T(8,128)(2,1)S(1)}, bf16[448,1024]{1,0:T(8,128)(2,1)S(1)}, u32[]{:S(2)}, u32[]{:S(2)}) collective-permute-start(bf16[448,1024]{1,0:T(8,128)(2,1)S(1)} %slice.279), channel_id=1, source_target_pairs={{0,2},{1,3},{2,0},{3,1},{4,6},{5,7},{6,4},{7,5},{8,10},{9,11},{10,... | collective-permute-start | bytes 2752520 | tf_op jit(solution)/shard_map/ppermute | solution.py:833
  64.5 8.4 %collective-permute-start.14 = (bf16[512,256]{1,0:T(8,128)(2,1)S(1)}, bf16[512,256]{1,0:T(8,128)(2,1)S(1)}, u32[]{:S(2)}, u32[]{:S(2)}) collective-permute-start(bf16[512,256]{1,0:T(8,128)(2,1)S(1)} %get-tuple-element.236), channel_id=1, source_target_pairs={{0,3},{1,2},{2,1},{3,0},{4,7},{5,6},{6,5},{7,4},{8,11},{9,10},{10,... | collective-permute-start | bytes 786440 | tf_op jit(solution)/shard_map/ppermute | solution.py:833
  65.7 13.0 %collective-permute-start.13 = (bf16[512,256]{1,0:T(8,128)(2,1)S(1)}, bf16[512,256]{1,0:T(8,128)(2,1)S(1)}, u32[]{:S(2)}, u32[]{:S(2)}) collective-permute-start(bf16[512,256]{1,0:T(8,128)(2,1)S(1)} %get-tuple-element.237), channel_id=1, source_target_pairs={{0,2},{1,3},{2,0},{3,1},{4,6},{5,7},{6,4},{7,5},{8,10},{9,11},{10,... | collective-permute-start | bytes 786440 | tf_op jit(solution)/shard_map/ppermute | solution.py:833
  66.2 12.5 %collective-permute-start.12 = (bf16[512,256]{1,0:T(8,128)(2,1)S(1)}, bf16[512,256]{1,0:T(8,128)(2,1)S(1)}, u32[]{:S(2)}, u32[]{:S(2)}) collective-permute-start(bf16[512,256]{1,0:T(8,128)(2,1)S(1)} %get-tuple-element.238), channel_id=1, source_target_pairs={{0,1},{1,0},{2,3},{3,2},{4,5},{5,4},{6,7},{7,6},{8,9},{9,8},{10,11... | collective-permute-start | bytes 786440 | tf_op jit(solution)/shard_map/ppermute | solution.py:833
  82.2 25.6 %collective-permute-start.18 = (bf16[512,1024]{1,0:T(8,128)(2,1)S(1)}, bf16[512,1024]{1,0:T(8,128)(2,1)S(1)}, u32[]{:S(2)}, u32[]{:S(2)}) collective-permute-start(bf16[512,1024]{1,0:T(8,128)(2,1)S(1)} %get-tuple-element.128.normed.refs_0_), channel_id=1, source_target_pairs={{0,2},{1,3},{2,0},{3,1},{4,6},{5,7},{6,4},{7,5},{8,10},{9,11},{10,... | collective-permute-start | bytes 3145736 | tf_op jit(solution)/shard_map/ppermute | solution.py:833
  91.3 16.6 %collective-permute-start.20 = (bf16[512,1024]{1,0:T(8,128)(2,1)}, bf16[512,1024]{1,0:T(8,128)(2,1)}, u32[]{:S(2)}, u32[]{:S(2)}) collective-permute-start(bf16[512,1024]{1,0:T(8,128)(2,1)} %get-tuple-element.138), channel_id=1, source_target_pairs={{0,1},{1,0},{2,3},{3,2},{4,5},{5,4},{6,7},{7,6},{8,9},{9,8},{10,11... | collective-permute-start | bytes 3145736 | tf_op jit(solution)/shard_map/ppermute | solution.py:833
  91.4 18.1 %collective-permute-start.17 = (bf16[512,1024]{1,0:T(8,128)(2,1)S(1)}, bf16[512,1024]{1,0:T(8,128)(2,1)}, u32[]{:S(2)}, u32[]{:S(2)}) collective-permute-start(bf16[512,1024]{1,0:T(8,128)(2,1)S(1)} %get-tuple-element.130), channel_id=1, source_target_pairs={{0,1},{1,0},{2,3},{3,2},{4,5},{5,4},{6,7},{7,6},{8,9},{9,8},{10,11... | collective-permute-start | bytes 3145736 | tf_op jit(solution)/shard_map/ppermute | solution.py:833
  122.8 36.2 %collective-permute-start.30 = (bf16[512,1024]{1,0:T(8,128)(2,1)}, bf16[512,1024]{1,0:T(8,128)(2,1)S(1)}, u32[]{:S(2)}, u32[]{:S(2)}) collective-permute-start(bf16[512,1024]{1,0:T(8,128)(2,1)} %get-tuple-element.164), channel_id=1, source_target_pairs={{0,1},{1,0},{2,3},{3,2},{4,5},{5,4},{6,7},{7,6},{8,9},{9,8},{10,11... | collective-permute-start | bytes 3145736 | tf_op jit(solution)/shard_map/ppermute | solution.py:833
  123.3 25.6 %collective-permute-start.23 = (bf16[512,1024]{1,0:T(8,128)(2,1)S(1)}, bf16[512,1024]{1,0:T(8,128)(2,1)S(1)}, u32[]{:S(2)}, u32[]{:S(2)}) collective-permute-start(bf16[512,1024]{1,0:T(8,128)(2,1)S(1)} %add_convert_fusion.3), channel_id=1, source_target_pairs={{0,2},{1,3},{2,0},{3,1},{4,6},{5,7},{6,4},{7,5},{8,10},{9,11},{10,... | collective-permute-start | bytes 3145736 | tf_op jit(solution)/shard_map/ppermute | solution.py:833
  132.5 27.0 %collective-permute-start.31 = (bf16[512,1024]{1,0:T(8,128)(2,1)S(1)}, bf16[512,1024]{1,0:T(8,128)(2,1)S(1)}, u32[]{:S(2)}, u32[]{:S(2)}) collective-permute-start(bf16[512,1024]{1,0:T(8,128)(2,1)S(1)} %get-tuple-element.150), channel_id=1, source_target_pairs={{0,8},{4,12},{8,0},{12,4},{16,24},{20,28},{24,16},{28,20},{1,9},{5... | collective-permute-start | bytes 3145736 | tf_op jit(solution)/shard_map/ppermute | solution.py:833
  134.2 34.4 %collective-permute-start.22 = (bf16[512,1024]{1,0:T(8,128)(2,1)S(1)}, bf16[512,1024]{1,0:T(8,128)(2,1)S(1)}, u32[]{:S(2)}, u32[]{:S(2)}) collective-permute-start(bf16[512,1024]{1,0:T(8,128)(2,1)S(1)} %get-tuple-element.145), channel_id=1, source_target_pairs={{0,4},{4,0},{8,12},{12,8},{16,20},{20,16},{24,28},{28,24},{1,5},{5... | collective-permute-start | bytes 3145736 | tf_op jit(solution)/shard_map/ppermute | solution.py:833
  154.6 9.1 %collective-permute-start.25 = (bf16[512,256]{1,0:T(8,128)(2,1)S(1)}, bf16[512,256]{1,0:T(8,128)(2,1)S(1)}, u32[]{:S(2)}, u32[]{:S(2)}) collective-permute-start(bf16[512,256]{1,0:T(8,128)(2,1)S(1)} %get-tuple-element.155), channel_id=1, source_target_pairs={{0,2},{1,3},{2,0},{3,1},{4,6},{5,7},{6,4},{7,5},{8,10},{9,11},{10,... | collective-permute-start | bytes 786440 | tf_op jit(solution)/shard_map/ppermute | solution.py:833
  159.0 9.5 %collective-permute-start.26 = (bf16[512,256]{1,0:T(8,128)(2,1)S(1)}, bf16[512,256]{1,0:T(8,128)(2,1)S(1)}, u32[]{:S(2)}, u32[]{:S(2)}) collective-permute-start(bf16[512,256]{1,0:T(8,128)(2,1)S(1)} %get-tuple-element.156), channel_id=1, source_target_pairs={{0,3},{1,2},{2,1},{3,0},{4,7},{5,6},{6,5},{7,4},{8,11},{9,10},{10,... | collective-permute-start | bytes 786440 | tf_op jit(solution)/shard_map/ppermute | solution.py:833
  159.5 12.0 %collective-permute-start.28 = (bf16[256,1024]{1,0:T(8,128)(2,1)S(1)}, bf16[256,1024]{1,0:T(8,128)(2,1)S(1)}, u32[]{:S(2)}, u32[]{:S(2)}) collective-permute-start(bf16[256,1024]{1,0:T(8,128)(2,1)S(1)} %get-tuple-element.160), channel_id=1, source_target_pairs={{0,1},{1,0},{2,3},{3,2},{4,5},{5,4},{6,7},{7,6},{8,9},{9,8},{10,11... | collective-permute-start | bytes 1572872 | tf_op jit(solution)/shard_map/ppermute | solution.py:833
  160.2 11.5 %collective-permute-start.29 = (bf16[256,1024]{1,0:T(8,128)(2,1)S(1)}, bf16[256,1024]{1,0:T(8,128)(2,1)S(1)}, u32[]{:S(2)}, u32[]{:S(2)}) collective-permute-start(bf16[256,1024]{1,0:T(8,128)(2,1)S(1)} %get-tuple-element.162), channel_id=1, source_target_pairs={{0,1},{1,0},{2,3},{3,2},{4,5},{5,4},{6,7},{7,6},{8,9},{9,8},{10,11... | collective-permute-start | bytes 1572872 | tf_op jit(solution)/shard_map/ppermute | solution.py:833
  169.5 28.2 %collective-permute-start.33 = (bf16[256,1024]{1,0:T(8,128)(2,1)S(1)}, bf16[256,1024]{1,0:T(8,128)(2,1)S(1)}, u32[]{:S(2)}, u32[]{:S(2)}) collective-permute-start(bf16[256,1024]{1,0:T(8,128)(2,1)S(1)} %get-tuple-element.226), channel_id=1, source_target_pairs={{0,16},{4,20},{8,24},{12,28},{16,0},{20,4},{24,8},{28,12},{1,17},{... | collective-permute-start | bytes 1572872 | tf_op jit(solution)/shard_map/ppermute | solution.py:833
  169.9 28.0 %collective-permute-start.27 = (bf16[256,1024]{1,0:T(8,128)(2,1)S(1)}, bf16[256,1024]{1,0:T(8,128)(2,1)S(1)}, u32[]{:S(2)}, u32[]{:S(2)}) collective-permute-start(bf16[256,1024]{1,0:T(8,128)(2,1)S(1)} %get-tuple-element.258), channel_id=1, source_target_pairs={{0,8},{4,12},{8,0},{12,4},{16,24},{20,28},{24,16},{28,20},{1,9},{5... | collective-permute-start | bytes 1572872 | tf_op jit(solution)/shard_map/ppermute | solution.py:833
  171.9 35.3 %collective-permute-start.34 = (bf16[256,1024]{1,0:T(8,128)(2,1)S(1)}, bf16[256,1024]{1,0:T(8,128)(2,1)S(1)}, u32[]{:S(2)}, u32[]{:S(2)}) collective-permute-start(bf16[256,1024]{1,0:T(8,128)(2,1)S(1)} %add_convert_fusion.15), channel_id=1, source_target_pairs={{0,2},{1,3},{2,0},{3,1},{4,6},{5,7},{6,4},{7,5},{8,10},{9,11},{10,... | collective-permute-start | bytes 1572872 | tf_op jit(solution)/shard_map/ppermute | solution.py:833
  173.5 58.9 %collective-permute-start.38 = (bf16[512,1024]{1,0:T(8,128)(2,1)S(1)}, bf16[512,1024]{1,0:T(8,128)(2,1)S(1)}, u32[]{:S(2)}, u32[]{:S(2)}) collective-permute-start(bf16[512,1024]{1,0:T(8,128)(2,1)S(1)} %add_convert_fusion.2), channel_id=1, source_target_pairs={{0,2},{1,3},{2,0},{3,1},{4,6},{5,7},{6,4},{7,5},{8,10},{9,11},{10,... | collective-permute-start | bytes 3145736 | tf_op jit(solution)/shard_map/ppermute | solution.py:833
  197.9 30.8 %collective-permute-start.35 = (bf16[256,1024]{1,0:T(8,128)(2,1)S(1)}, bf16[256,1024]{1,0:T(8,128)(2,1)S(1)}, u32[]{:S(2)}, u32[]{:S(2)}) collective-permute-start(bf16[256,1024]{1,0:T(8,128)(2,1)S(1)} %pad_maximum_fusion.6), channel_id=1, source_target_pairs={{0,4},{4,0},{8,12},{12,8},{16,20},{20,16},{24,28},{28,24},{1,5},{5... | collective-permute-start | bytes 1572872 | tf_op jit(solution)/shard_map/ppermute | solution.py:833
  198.3 31.0 %collective-permute-start.32 = (bf16[256,1024]{1,0:T(8,128)(2,1)S(1)}, bf16[256,1024]{1,0:T(8,128)(2,1)S(1)}, u32[]{:S(2)}, u32[]{:S(2)}) collective-permute-start(bf16[256,1024]{1,0:T(8,128)(2,1)S(1)} %pad_maximum_fusion.5), channel_id=1, source_target_pairs={{0,16},{4,20},{8,24},{12,28},{16,0},{20,4},{24,8},{28,12},{1,17},{... | collective-permute-start | bytes 1572872 | tf_op jit(solution)/shard_map/ppermute | solution.py:833
  207.1 20.8 %collective-permute-start.37 = (bf16[192,1024]{1,0:T(8,128)(2,1)S(1)}, bf16[192,1024]{1,0:T(8,128)(2,1)S(1)}, u32[]{:S(2)}, u32[]{:S(2)}) collective-permute-start(bf16[192,1024]{1,0:T(8,128)(2,1)S(1)} %get-tuple-element.177), channel_id=1, source_target_pairs={{0,8},{4,12},{8,0},{12,4},{16,24},{20,28},{24,16},{28,20},{1,9},{5... | collective-permute-start | bytes 1179656 | tf_op jit(solution)/shard_map/ppermute | solution.py:833
  213.2 18.0 %collective-permute-start.36 = (bf16[320,1024]{1,0:T(8,128)(2,1)S(1)}, bf16[320,1024]{1,0:T(8,128)(2,1)S(1)}, u32[]{:S(2)}, u32[]{:S(2)}) collective-permute-start(bf16[320,1024]{1,0:T(8,128)(2,1)S(1)} %bitcast.81), channel_id=1, source_target_pairs={{0,4},{4,0},{8,12},{12,8},{16,20},{20,16},{24,28},{28,24},{1,5},{5... | collective-permute-start | bytes 1966088 | tf_op jit(solution)/shard_map/ppermute | solution.py:833
  227.9 8.8 %collective-permute-start.39 = (bf16[512,1024]{1,0:T(8,128)(2,1)}, bf16[512,1024]{1,0:T(8,128)(2,1)}, u32[]{:S(2)}, u32[]{:S(2)}) collective-permute-start(bf16[512,1024]{1,0:T(8,128)(2,1)} %get-tuple-element.188), channel_id=1, source_target_pairs={{0,1},{1,0},{2,3},{3,2},{4,5},{5,4},{6,7},{7,6},{8,9},{9,8},{10,11... | collective-permute-start | bytes 3145736 | tf_op jit(solution)/shard_map/ppermute | solution.py:833
  228.8 9.2 %collective-permute-start.40 = (bf16[512,1024]{1,0:T(8,128)(2,1)}, bf16[512,1024]{1,0:T(8,128)(2,1)}, u32[]{:S(2)}, u32[]{:S(2)}) collective-permute-start(bf16[512,1024]{1,0:T(8,128)(2,1)} %get-tuple-element.191), channel_id=1, source_target_pairs={{0,1},{1,0},{2,3},{3,2},{4,5},{5,4},{6,7},{7,6},{8,9},{9,8},{10,11... | collective-permute-start | bytes 3145736 | tf_op jit(solution)/shard_map/ppermute | solution.py:833
  235.4 10.1 %collective-permute-start.47 = (bf16[96,1024]{1,0:T(8,128)(2,1)}, bf16[96,1024]{1,0:T(8,128)(2,1)}, u32[]{:S(2)}, u32[]{:S(2)}) collective-permute-start(bf16[96,1024]{1,0:T(8,128)(2,1)} %get-tuple-element.240), channel_id=1, source_target_pairs={{0,4},{4,0},{8,12},{12,8},{16,20},{20,16},{24,28},{28,24},{1,5},{5... | collective-permute-start | bytes 589832 | tf_op jit(solution)/shard_map/ppermute | solution.py:833
  235.8 32.5 %collective-permute-start.44 = (bf16[256,1024]{1,0:T(8,128)(2,1)}, bf16[256,1024]{1,0:T(8,128)(2,1)}, u32[]{:S(2)}, u32[]{:S(2)}) collective-permute-start(bf16[256,1024]{1,0:T(8,128)(2,1)} %add_convert_fusion.11), channel_id=1, source_target_pairs={{0,8},{4,12},{8,0},{12,4},{16,24},{20,28},{24,16},{28,20},{1,9},{5... | collective-permute-start | bytes 1572872 | tf_op jit(solution)/shard_map/ppermute | solution.py:833
  236.6 31.6 %collective-permute-start.45 = (bf16[256,1024]{1,0:T(8,128)(2,1)}, bf16[256,1024]{1,0:T(8,128)(2,1)}, u32[]{:S(2)}, u32[]{:S(2)}) collective-permute-start(bf16[256,1024]{1,0:T(8,128)(2,1)} %add_convert_fusion.10), channel_id=1, source_target_pairs={{0,16},{4,20},{8,24},{12,28},{16,0},{20,4},{24,8},{28,12},{1,17},{... | collective-permute-start | bytes 1572872 | tf_op jit(solution)/shard_map/ppermute | solution.py:833
  236.7 31.6 %collective-permute-start.46 = (bf16[160,1024]{1,0:T(8,128)(2,1)}, bf16[160,1024]{1,0:T(8,128)(2,1)S(1)}, u32[]{:S(2)}, u32[]{:S(2)}) collective-permute-start(bf16[160,1024]{1,0:T(8,128)(2,1)} %get-tuple-element.230), channel_id=1, source_target_pairs={{0,8},{4,12},{8,0},{12,4},{16,24},{20,28},{24,16},{28,20},{1,9},{5... | collective-permute-start | bytes 983048 | tf_op jit(solution)/shard_map/ppermute | solution.py:833
  237.9 6.0 %collective-permute-start.43 = (f32[96,128]{1,0:T(8,128)S(1)}, f32[96,128]{1,0:T(8,128)S(1)}, u32[]{:S(2)}, u32[]{:S(2)}) collective-permute-start(f32[96,128]{1,0:T(8,128)S(1)} %pad_maximum_fusion.13), channel_id=1, source_target_pairs={{0,4},{4,0},{8,12},{12,8},{16,20},{20,16},{24,28},{28,24},{1,5},{5... | collective-permute-start | bytes 147464 | tf_op jit(solution)/shard_map/ppermute | solution.py:833
  244.0 31.7 %collective-permute-start.41 = (bf16[512,1024]{1,0:T(8,128)(2,1)S(1)}, bf16[512,1024]{1,0:T(8,128)(2,1)S(1)}, u32[]{:S(2)}, u32[]{:S(2)}) collective-permute-start(bf16[512,1024]{1,0:T(8,128)(2,1)S(1)} %add_convert_fusion), channel_id=1, source_target_pairs={{0,2},{1,3},{2,0},{3,1},{4,6},{5,7},{6,4},{7,5},{8,10},{9,11},{10,... | collective-permute-start | bytes 3145736 | tf_op jit(solution)/shard_map/ppermute | solution.py:833
  268.3 12.9 %collective-permute-start.48 = (f32[80,128]{1,0:T(8,128)S(1)}, f32[80,128]{1,0:T(8,128)S(1)}, u32[]{:S(2)}, u32[]{:S(2)}) collective-permute-start(f32[80,128]{1,0:T(8,128)S(1)} %slice.292), channel_id=1, source_target_pairs={{0,2},{1,3},{2,0},{3,1},{4,6},{5,7},{6,4},{7,5},{8,10},{9,11},{10,... | collective-permute-start | bytes 122888 | tf_op jit(solution)/shard_map/ppermute | solution.py:833
  271.0 41.1 %collective-permute-start.50 = (bf16[512,1024]{1,0:T(8,128)(2,1)S(1)}, bf16[512,1024]{1,0:T(8,128)(2,1)S(1)}, u32[]{:S(2)}, u32[]{:S(2)}) collective-permute-start(bf16[512,1024]{1,0:T(8,128)(2,1)S(1)} %pad_maximum_fusion.1.first), channel_id=1, source_target_pairs={{0,4},{4,0},{8,12},{12,8},{16,20},{20,16},{24,28},{28,24},{1,5},{5... | collective-permute-start | bytes 3145736 | tf_op jit(solution)/shard_map/ppermute | solution.py:833
  274.1 38.1 %collective-permute-start.53 = (bf16[512,1024]{1,0:T(8,128)(2,1)S(1)}, bf16[512,1024]{1,0:T(8,128)(2,1)S(1)}, u32[]{:S(2)}, u32[]{:S(2)}) collective-permute-start(bf16[512,1024]{1,0:T(8,128)(2,1)S(1)} %pad_maximum_fusion.2.first), channel_id=1, source_target_pairs={{0,8},{4,12},{8,0},{12,4},{16,24},{20,28},{24,16},{28,20},{1,9},{5... | collective-permute-start | bytes 3145736 | tf_op jit(solution)/shard_map/ppermute | solution.py:833
  275.6 26.7 %collective-permute-start.52 = (bf16[96,1024]{1,0:T(8,128)(2,1)S(1)}, bf16[96,1024]{1,0:T(8,128)(2,1)S(1)}, u32[]{:S(2)}, u32[]{:S(2)}) collective-permute-start(bf16[96,1024]{1,0:T(8,128)(2,1)S(1)} %pad_maximum_fusion.10), channel_id=1, source_target_pairs={{0,16},{4,20},{8,24},{12,28},{16,0},{20,4},{24,8},{28,12},{1,17},{... | collective-permute-start | bytes 589832 | tf_op jit(solution)/shard_map/ppermute | solution.py:833
  275.7 33.6 %collective-permute-start.51 = (bf16[160,1024]{1,0:T(8,128)(2,1)S(1)}, bf16[160,1024]{1,0:T(8,128)(2,1)S(1)}, u32[]{:S(2)}, u32[]{:S(2)}) collective-permute-start(bf16[160,1024]{1,0:T(8,128)(2,1)S(1)} %pad_maximum_fusion.9), channel_id=1, source_target_pairs={{0,16},{4,20},{8,24},{12,28},{16,0},{20,4},{24,8},{28,12},{1,17},{... | collective-permute-start | bytes 983048 | tf_op jit(solution)/shard_map/ppermute | solution.py:833
  281.2 36.6 %collective-permute-start.49 = (f32[96,128]{1,0:T(8,128)S(1)}, f32[96,128]{1,0:T(8,128)S(1)}, u32[]{:S(2)}, u32[]{:S(2)}) collective-permute-start(f32[96,128]{1,0:T(8,128)S(1)} %pad_maximum_fusion.14), channel_id=1, source_target_pairs={{0,16},{4,20},{8,24},{12,28},{16,0},{20,4},{24,8},{28,12},{1,17},{... | collective-permute-start | bytes 147464 | tf_op jit(solution)/shard_map/ppermute | solution.py:833
  309.4 8.4 %collective-permute-start.55 = (bf16[160,1024]{1,0:T(8,128)(2,1)S(1)}, bf16[160,1024]{1,0:T(8,128)(2,1)S(1)}, u32[]{:S(2)}, u32[]{:S(2)}) collective-permute-start(bf16[160,1024]{1,0:T(8,128)(2,1)S(1)} %add_convert_fusion.19), channel_id=1, source_target_pairs={{0,8},{4,12},{8,0},{12,4},{16,24},{20,28},{24,16},{28,20},{1,9},{5... | collective-permute-start | bytes 983048 | tf_op jit(solution)/shard_map/ppermute | solution.py:833
  309.6 15.1 %collective-permute-start.57 = (bf16[96,1024]{1,0:T(8,128)(2,1)S(1)}, bf16[96,1024]{1,0:T(8,128)(2,1)S(1)}, u32[]{:S(2)}, u32[]{:S(2)}) collective-permute-start(bf16[96,1024]{1,0:T(8,128)(2,1)S(1)} %add_convert_fusion.24), channel_id=1, source_target_pairs={{0,4},{4,0},{8,12},{12,8},{16,20},{20,16},{24,28},{28,24},{1,5},{5... | collective-permute-start | bytes 589832 | tf_op jit(solution)/shard_map/ppermute | solution.py:833
  317.9 15.4 %collective-permute-start.56 = (bf16[320,1024]{1,0:T(8,128)(2,1)S(1)}, bf16[320,1024]{1,0:T(8,128)(2,1)S(1)}, u32[]{:S(2)}, u32[]{:S(2)}) collective-permute-start(bf16[320,1024]{1,0:T(8,128)(2,1)S(1)} %pad_maximum_fusion.4.first), channel_id=1, source_target_pairs={{0,4},{4,0},{8,12},{12,8},{16,20},{20,16},{24,28},{28,24},{1,5},{5... | collective-permute-start | bytes 1966088 | tf_op jit(solution)/shard_map/ppermute | solution.py:833
  324.7 7.8 %collective-permute-start.58 = (bf16[192,1024]{1,0:T(8,128)(2,1)S(1)}, bf16[192,1024]{1,0:T(8,128)(2,1)S(1)}, u32[]{:S(2)}, u32[]{:S(2)}) collective-permute-start(bf16[192,1024]{1,0:T(8,128)(2,1)S(1)} %pad_maximum_fusion.7.first), channel_id=1, source_target_pairs={{0,8},{4,12},{8,0},{12,4},{16,24},{20,28},{24,16},{28,20},{1,9},{5... | collective-permute-start | bytes 1179656 | tf_op jit(solution)/shard_map/ppermute | solution.py:833
  (44 other events, 369.1 us)
where the time goes:
time: 344 us; the launch traced here: 337 us
  waiting for transfers between devices  135 us (39%)
  Pallas kernels  116 us (34%)
  starting transfers between devices  48.3 us (14%)
  other arithmetic  24.2 us (7%)
  local copies, waits for them, and re-layouts  7.86 us (2%)
  matrix products  4.12 us (1%)
    ppermute x59, waiting for transfers between devices, swap(): lax.ppermute(array, axis, [(i, i ^ bit) for i in range(lax.axis_size(axis...  135 us
    ppermute x59, starting transfers between devices, swap(): lax.ppermute(array, axis, [(i, i ^ bit) for i in range(lax.axis_size(axis...  48.3 us
    pallas_call x1, Pallas kernels, attend_back(): call(body, (1,), [scalars(), scalars()] + [whole(piece.shape) for piece i...  23.7 us
    pallas_call x4, Pallas kernels, feed(): call(feed_body, (rows // tile,), [block, block, whole(w_up.shape), whole(...  22.9 us
    pallas_call x5, Pallas kernels, outer(): call(functools.partial(outer_body, found, 256, count, len(base)), (1,), [...  18.6 us
    pallas_call x1, Pallas kernels, attend(): call(body, (1,), [scalars(), scalars()] + [whole((own_rows, width3))] * l...  17.2 us
    convert_element_type x20, other arithmetic, add(): return (left.astype(F32) + right.astype(F32)).astype(left.dtype)  14.8 us
    pallas_call x5, Pallas kernels, unpack(): call(functools.partial(unpack_body, bits, sections), (1,), [scalars(), wh...  8.61 us
  transfers between devices with their start and end apart: 59, of which 23 were waited for; matrix products, arithmetic and copies ran while one was open for 8% of the time, Pallas kernels for 31%

commit v1 on v0

--- a/solution.py
+++ b/solution.py
@@ -497,7 +497,7 @@
     )(lengths, place, *mixed, *weights, stream0, shift, gain, bias)
 
 
-def feed_body(normed, grad_mlp, w_up, up_bias, w_down, act_out, upin_out, mlp_out, norm_out, bias_out):
+def feed_body(normed, grad_mlp, w_up, up_bias, w_down, act_out, upin_out, norm_out, bias_out, *mlp_out):
     hidden = w_up.shape[1]
     chunk = min(512, hidden)
     left, grad = normed[...], grad_mlp[...]
@@ -525,15 +525,17 @@
         act_out[:, here] = act
         upin_out[:, here] = upin
         bias_out[:, here] += column_sum(upin.astype(F32))
-        mlp_part = mxu(act, w_down[here, :], NN)
         norm_part = mxu(upin, w_up[:, here], NT)
-        mlp = mlp_part if mlp is None else mlp + mlp_part
         norm = norm_part if norm is None else norm + norm_part
-    mlp_out[...] = mlp.astype(BF16)
+        if mlp_out:
+            mlp_part = mxu(act, w_down[here, :], NN)
+            mlp = mlp_part if mlp is None else mlp + mlp_part
     norm_out[...] = norm.astype(BF16)
-
-
-def feed(normed, grad_mlp, w_up, up_bias, w_down):
+    if mlp_out:
+        mlp_out[0][...] = mlp.astype(BF16)
+
+
+def feed(normed, grad_mlp, w_up, up_bias, w_down, with_mlp):
     rows, width = normed.shape
     hidden = w_up.shape[1]
     tile = min(512, rows)
@@ -543,14 +545,14 @@
         feed_body,
         (rows // tile,),
         [block, block, whole(w_up.shape), whole((1, hidden)), whole(w_down.shape)],
-        [wide, wide, block, block, whole((1, hidden))],
+        [wide, wide, block, whole((1, hidden))] + [block] * with_mlp,
         [
             like((rows, hidden), BF16),
             like((rows, hidden), BF16),
             like((rows, width), BF16),
-            like((rows, width), BF16),
             like((1, hidden), F32),
-        ],
+        ]
+        + [like((rows, width), BF16)] * with_mlp,
         8 * rows * width * hidden,
         12 * rows * width + 4 * width * hidden,
         limit=24,
@@ -689,6 +691,29 @@
     )(place, first, second)
 
 
+def join_body(bits_a, sections_a, bits_b, sections_b, place, *refs):
+    joined, rows = refs[4], sections_a[0]
+    unpack_body(bits_a, sections_a, place, refs[0], refs[1], joined.at[:rows], *refs[5:])
+    unpack_body(bits_b, sections_b, place, refs[2], refs[3], joined.at[rows:])
+
+
+def join(place, chain_a, chain_b):
+    halves = [chain_a.kept, chain_a.came, chain_b.kept, chain_b.came]
+    width = halves[0].shape[1]
+    outs = [chain_a.sections[0] + chain_b.sections[0], *chain_a.sections[1:]]
+    return call(
+        functools.partial(
+            join_body, chain_a.bits[:-1], chain_a.sections, chain_b.bits[:-1], chain_b.sections
+        ),
+        (1,),
+        [scalars()] + [whole(half.shape) for half in halves],
+        [whole((rows, width)) for rows in outs],
+        [like((rows, width), F32) for rows in outs],
+        0,
+        0,
+    )(place, *halves)
+
+
 def project_body(group_count, piece_count, *refs):
     grads = refs[:group_count]
     weights = refs[group_count : 2 * group_count]
@@ -994,15 +1019,15 @@
 
     normed2_far = swap(normed2_own, "mp", top)
     normed2 = spread(normed2_own, top)
-    fed = [feed(normed2[p], grad_mlp[p], w_up, up_shift, w_down) for p in range(top)]
+    fed = [feed(normed2[p], grad_mlp[p], w_up, up_shift, w_down, True) for p in range(top)]
     [[down_base]] = outer(place, [f[0] for f in fed], grad_mlp[:top], [(w_down.shape[0], [])], dtype=F32)
     [[up_base]] = outer(place, normed2, [f[1] for f in fed], [(width, [])], dtype=F32)
     far_normed = spread(after(normed2_far, down_base, up_base), top)
-    norm2_near, mlp_near = fold([f[3] for f in fed]), fold([f[2] for f in fed])
+    norm2_near, mlp_near = fold([f[2] for f in fed]), fold([f[4] for f in fed])
     far_normed[-1] = after(far_normed[-1], norm2_near, mlp_near)
     right = grad_mlp[top:]
-    far_fed = [feed(n, g, w_up, up_shift, w_down) for n, g in zip(far_normed, right)]
-    norm2_part = fold([f[3] for f in far_fed])
+    far_fed = [feed(n, g, w_up, up_shift, w_down, False) for n, g in zip(far_normed, right)]
+    norm2_part = fold([f[2] for f in far_fed])
     norm2_far = swap(norm2_part, "mp", top)
     acts, upins = [f[0] for f in far_fed], [f[1] for f in far_fed]
     acts[-1] = after(acts[-1], norm2_part)
@@ -1011,8 +1036,9 @@
     upins[-1] = after(upins[-1], *down_halves)
     [up_halves] = outer(place, far_normed, upins, [(width, low_last[:-1])], [up_base])
     grad_up = DpSum(place, [up_halves], low_last)
-    grad_up_bias = functools.reduce(jnp.add, [f[4] for f in fed + far_fed])
-    norm2_far = after(norm2_far, *up_halves)
+    grad_up_bias = functools.reduce(jnp.add, [f[3] for f in fed + far_fed])
+    mlp_parts = [mxu(after(f[0], *up_halves), w_down, NN).astype(BF16) for f in far_fed]
+    norm2_far = after(norm2_far, *mlp_parts)
     grad_stream1, grad_attn, grad_mixed, second_sums = second_back(
         lengths, place, norm2_near, norm2_far, stream1, cotangent, gain2, w_out_all
     )
@@ -1020,18 +1046,17 @@
     grads = exchange(list(grad_mixed))
     out_parts = outer_each(place, mixed, grad_attn, low_first[:-1])
     out_near, out_part = fold(out_parts[:top]), fold(out_parts[top:])
-    mlp_part = fold([f[2] for f in far_fed])
     now = advance([grad_down, grad_up], grads)
-    grads[-1] = after(grads[-1], out_near, out_part, mlp_part, *now)
+    grads[-1] = after(grads[-1], out_near, out_part, *now)
     out_far = swap(after(out_part, grads[-1]), "mp", top)
-    mlp_far = swap(after(mlp_part, grads[-1]), "mp", top)
     proj, proj_sums = attend_back(lengths, place, qkv, grads, attended, logsum, 0, heads)
+    mlp_far = swap(fold(mlp_parts, proj), "mp", top)
     now = advance([grad_down, grad_up], [proj])
     qkv_rows = 3 * depth // 2
     halves_a, halves_b = outer(
         place, [after(proj, *now)], normed1, [(qkv_rows, low_first[:-1]), (qkv_rows, low_second[:-1])]
     )
-    out_far = after(out_far, *halves_a)
+    out_far = after(out_far, proj)
     out_sum = add(out_near, out_far)
     groups_a = [halves_a]
     if len(halves_a) > 1 and splits(depth, low_first[:-1]):
@@ -1079,9 +1104,12 @@
         flat = hop(flat, "dp", dp_hops, grad_down, grad_up)
         now = advance(proj_chains, [grad_down, grad_up, flat])
 
-    grad_a, grad_b = grad_a.done(), grad_b.done()
-    grad_out_weight = grad_a[1] if len(grad_a) > 1 else lax.psum(out_sum, "dp").astype(F32)
-    grad_qkv = jnp.concatenate([grad_a[0], grad_b[0]], axis=0).reshape(3, depth, width)
+    if hasattr(grad_a, "came") and hasattr(grad_b, "came"):
+        grad_qkv, *others = join(place, grad_a, grad_b)
+    else:
+        grad_qkv, others = jnp.concatenate([grad_a.done()[0], grad_b.done()[0]], axis=0), []
+    grad_qkv = grad_qkv.reshape(3, depth, width)
+    grad_out_weight = others[0] if others else lax.psum(out_sum, "dp").astype(F32)
     flat = flat.reshape(-1)
     rows = flat[: rows.size].reshape(rows.shape)
     up_sums = flat[rows.size : rows.size + up_bias.shape[0]]

time: 344 us -> 342 us (level)
  starting transfers between devices: 48.3 us -> 72.2 us
  Pallas kernels: 116 us -> 102 us
  waiting for transfers between devices: 135 us -> 124 us
    ppermute x59, starting transfers between devices: 48.3 us -> 72.2 us  [swap(): lax.ppermute(array, axis, [(i, i ^ bit) for i in range(lax.axis_size(axis...]
    ppermute x59, waiting for transfers between devices: 135 us -> 124 us  [swap(): lax.ppermute(array, axis, [(i, i ^ bit) for i in range(lax.axis_size(axis...]
    pallas_call x1, Pallas kernels: 23.7 us -> 16 us  [attend_back(): call(body, (1,), [scalars(), scalars()] + [whole(piece.shape) for piece i...]
    pallas_call x1, Pallas kernels: 17.2 us -> 12.5 us  [attend(): call(body, (1,), [scalars(), scalars()] + [whole((own_rows, width3))] * l...]
    pallas_call x5 -> x3, Pallas kernels: 8.61 us -> 6.29 us  [unpack(): call(functools.partial(unpack_body, bits, sections), (1,), [scalars(), wh...]
  transfers between devices with their start and end apart: 59 -> 59, of which waited for: 23 -> 22; matrix products, arithmetic and copies ran while one was open for 8% -> 9% of each run, Pallas kernels for 31% -> 27%
where the time goes in v1:
time: 342 us; the launch traced here: 337 us
  waiting for transfers between devices  124 us (36%)
  Pallas kernels  102 us (30%)
  starting transfers between devices  72.2 us (21%)
  other arithmetic  22.1 us (6%)
  local copies, waits for them, and re-layouts  6.84 us (2%)
  matrix products  6.66 us (2%)
    ppermute x59, waiting for transfers between devices, swap(): lax.ppermute(array, axis, [(i, i ^ bit) for i in range(lax.axis_size(axis...  124 us
    ppermute x59, starting transfers between devices, swap(): lax.ppermute(array, axis, [(i, i ^ bit) for i in range(lax.axis_size(axis...  72.2 us
    pallas_call x4, Pallas kernels, feed(): call(feed_body, (rows // tile,), [block, block, whole(w_up.shape), whole(...  21 us
    pallas_call x5, Pallas kernels, outer(): call(functools.partial(outer_body, found, 256, count, len(base)), (1,), [...  18.5 us
    pallas_call x1, Pallas kernels, attend_back(): call(body, (1,), [scalars(), scalars()] + [whole(piece.shape) for piece i...  16 us
    convert_element_type x20, other arithmetic, add(): return (left.astype(F32) + right.astype(F32)).astype(left.dtype)  14.8 us
    pallas_call x1, Pallas kernels, attend(): call(body, (1,), [scalars(), scalars()] + [whole((own_rows, width3))] * l...  12.5 us
  transfers between devices with their start and end apart: 59, of which 22 were waited for; matrix products, arithmetic and copies ran while one was open for 9% of the time, Pallas kernels for 27%

profile of v1, /device:TPU:0, one launch (start us, length us, event | category | flops | bytes accessed | tf_op | source)
XLA Modules:
  0.0 336.7 jit_solution(16500528332928589531)
XLA Ops:
  2.1 2.5 collective-permute-start
  9.2 3.3 shard_map.280
  12.7 2.9 collective-permute-start.4
  17.1 2.5 collective-permute-done.4
  20.5 4.2 %collective-permute-done.5 = bf16[64,1024]{1,0:T(8,128)(2,1)S(1)} collective-permute-done((bf16[64,1024]{1,0:T(8,128)(2,1)S(1)}, bf16[64,1024]{1,0:T(8,128)(2,1)S(1)}, u32[]{:S(2)}, u32[]{:S(2)}) %collective-permute-start.5) | collective-permute-done | bytes 131104 | tf_op jit(solution)/shard_map/ppermute | solution.py:858
  27.4 3.8 %collective-permute-done.6.second = bf16[128,1024]{1,0:T(8,128)(2,1)S(1)} collective-permute-done((bf16[128,1024]{1,0:T(8,128)(2,1)S(1)}, bf16[128,1024]{1,0:T(8,128)(2,1)S(1)}, u32[]{:S(2)}, u32[]{:S(2)}) %collective-permute-start.6) | collective-permute-done | bytes 262176 | tf_op jit(solution)/shard_map/ppermute | solution.py:858
  32.9 8.0 %collective-permute-done.3.refs_3_.refs_4_ = bf16[512,1024]{1,0:T(8,128)(2,1)S(1)} collective-permute-done((bf16[512,1024]{1,0:T(8,128)(2,1)S(1)}, bf16[512,1024]{1,0:T(8,128)(2,1)S(1)}, u32[]{:S(2)}, u32[]{:S(2)}) %collective-permute-start.3) | collective-permute-done | bytes 1048608 | tf_op jit(solution)/shard_map/ppermute | solution.py:858
  44.6 12.5 %shard_map.283 = (bf16[2048,256]{1,0:T(8,128)(2,1)S(1)}, f32[4,8,1,256]{3,2,1,0:T(1,128)S(1)}) custom-call(s32[5]{0:T(128)S(1)} %copy-done.21, s32[2]{0:T(128)S(1)} %pad_add_fusion.place.place_ref, bf16[512,768]{1,0:T(8,128)(2,1)S(1)} %add_convert_fusion.9.refs_0_, bf16[512,768]{1,0:T(8,128)(2,1)S(1)} %add_convert_fusion.8.refs_1_, ...), custom_call_target="tpu_custom_call" | custom-call | tf_op jit(solution)/shard_map/pallas_call | solution.py:317
  57.2 6.6 %collective-permute-done.10 = bf16[448,1024]{1,0:T(8,128)(2,1)S(1)} collective-permute-done((bf16[448,1024]{1,0:T(8,128)(2,1)S(1)}, bf16[448,1024]{1,0:T(8,128)(2,1)S(1)}, u32[]{:S(2)}, u32[]{:S(2)}) %collective-permute-start.10) | collective-permute-done | bytes 917536 | tf_op jit(solution)/shard_map/ppermute | solution.py:858
  67.3 5.6 %collective-permute-done.14.refs_3_ = bf16[512,256]{1,0:T(8,128)(2,1)S(1)} collective-permute-done((bf16[512,256]{1,0:T(8,128)(2,1)S(1)}, bf16[512,256]{1,0:T(8,128)(2,1)S(1)}, u32[]{:S(2)}, u32[]{:S(2)}) %collective-permute-start.14) | collective-permute-done | bytes 262176 | tf_op jit(solution)/shard_map/ppermute | solution.py:858
  72.9 5.9 %collective-permute-done.13.refs_2_ = bf16[512,256]{1,0:T(8,128)(2,1)S(1)} collective-permute-done((bf16[512,256]{1,0:T(8,128)(2,1)S(1)}, bf16[512,256]{1,0:T(8,128)(2,1)S(1)}, u32[]{:S(2)}, u32[]{:S(2)}) %collective-permute-start.13) | collective-permute-done | bytes 262176 | tf_op jit(solution)/shard_map/ppermute | solution.py:858
  78.8 3.3 shard_map.284
  84.9 5.8 %shard_map.286 = (bf16[512,1024]{1,0:T(8,128)(2,1)S(1)}, bf16[512,1024]{1,0:T(8,128)(2,1)S(1)}, bf16[512,1024]{1,0:T(8,128)(2,1)}, f32[1,1024]{1,0:T(1,128)S(1)}, bf16[512,1024]{1,0:T(8,128)(2,1)S(1)}) custom-call(bf16[512,1024]{1,0:T(8,128)(2,1)S(1)} %collective-permute-done.16.normed.refs_1_, ...), custom_call_target="tpu_custom_call" | custom-call | tf_op jit(solution)/shard_map/pallas_call | solution.py:544
  91.3 5.8 %shard_map.285 = (bf16[512,1024]{1,0:T(8,128)(2,1)S(1)}, bf16[512,1024]{1,0:T(8,128)(2,1)S(1)}, bf16[512,1024]{1,0:T(8,128)(2,1)S(1)}, f32[1,1024]{1,0:T(1,128)S(1)}, bf16[512,1024]{1,0:T(8,128)(2,1)S(1)}) custom-call(bf16[512,1024]{1,0:T(8,128)(2,1)S(1)} %get-tuple-element.128.normed.refs_0_, bf16[512,1024]{1,0:T(8,128)(2,1)S(1)} %shard_map.281.grad_mlp.refs_2_, ...), custom_call_target="tpu_custom_call" | custom-call | tf_op jit(solution)/shard_map/pallas_call | solution.py:544
  97.1 3.3 shard_map.287.refs_0_
  100.4 3.0 shard_map.288.refs_0_
  103.4 4.4 %collective-permute-done.18.normed.refs_1_ = bf16[512,1024]{1,0:T(8,128)(2,1)S(1)} collective-permute-done((bf16[512,1024]{1,0:T(8,128)(2,1)S(1)}, bf16[512,1024]{1,0:T(8,128)(2,1)S(1)}, u32[]{:S(2)}, u32[]{:S(2)}) %collective-permute-start.18) | collective-permute-done | bytes 1048608 | tf_op jit(solution)/shard_map/ppermute | solution.py:858
  111.1 4.7 %shard_map.290 = (bf16[512,1024]{1,0:T(8,128)(2,1)S(1)}, bf16[512,1024]{1,0:T(8,128)(2,1)S(1)}, bf16[512,1024]{1,0:T(8,128)(2,1)S(1)}, f32[1,1024]{1,0:T(1,128)S(1)}) custom-call(bf16[512,1024]{1,0:T(8,128)(2,1)S(1)} %collective-permute-done.19.normed.refs_2_, bf16[512,1024]{1,0:T(8,128)(2,1)S(1)} %collective-permute-done.11.grad_mlp.refs_4_, ...), custom_call_target="tpu_custom_call" | custom-call | tf_op jit(solution)/shard_map/pallas_call | solution.py:544
  116.4 4.7 %shard_map.289 = (bf16[512,1024]{1,0:T(8,128)(2,1)S(1)}, bf16[512,1024]{1,0:T(8,128)(2,1)S(1)}, bf16[512,1024]{1,0:T(8,128)(2,1)S(1)}, f32[1,1024]{1,0:T(1,128)S(1)}) custom-call(bf16[512,1024]{1,0:T(8,128)(2,1)S(1)} %collective-permute-done.18.normed.refs_1_, bf16[512,1024]{1,0:T(8,128)(2,1)S(1)} %constant_dynamic-update-slice_fusion.3.grad_mlp.refs_3_, ...), custom_call_target="tpu_custom_call" | custom-call | tf_op jit(solution)/shard_map/pallas_call | solution.py:544
  123.1 3.9 %shard_map.291 = (bf16[512,1024]{1,0:T(8,128)(2,1)S(1)}, bf16[512,1024]{1,0:T(8,128)(2,1)S(1)}) custom-call(s32[2]{0:T(128)S(1)} %pad_add_fusion.place.place_ref, f32[1024,1024]{1,0:T(8,128)S(1)} %shard_map.287.refs_0_, bf16[512,1024]{1,0:T(8,128)(2,1)S(1)} %get-tuple-element.151.refs_1_, bf16[512,1024]{1,0:T(8,128)(2,1)S(1)} %get-tuple-element.152.refs_2_, ...), custom_call_target="tpu_custom_call" | custom-call | tf_op jit(solution)/shard_map/pallas_call | solution.py:626
  127.0 3.7 %shard_map.292 = (bf16[512,1024]{1,0:T(8,128)(2,1)S(1)}, bf16[512,1024]{1,0:T(8,128)(2,1)S(1)}) custom-call(s32[2]{0:T(128)S(1)} %pad_add_fusion.place.place_ref, f32[1024,1024]{1,0:T(8,128)S(1)} %shard_map.288.refs_0_, bf16[512,1024]{1,0:T(8,128)(2,1)S(1)} %collective-permute-done.18.normed.refs_1_, ...), custom_call_target="tpu_custom_call" | custom-call | tf_op jit(solution)/shard_map/pallas_call | solution.py:626
  136.5 10.2 %collective-permute-done.23.half_b = bf16[512,1024]{1,0:T(8,128)(2,1)S(1)} collective-permute-done((bf16[512,1024]{1,0:T(8,128)(2,1)S(1)}, bf16[512,1024]{1,0:T(8,128)(2,1)S(1)}, u32[]{:S(2)}, u32[]{:S(2)}) %collective-permute-start.23) | collective-permute-done | bytes 1048608 | tf_op jit(solution)/shard_map/ppermute | solution.py:858
  146.7 4.3 %shard_map.293 = (f32[512,1024]{1,0:T(8,128)S(1)}, bf16[512,1024]{1,0:T(8,128)(2,1)S(1)}, bf16[512,256]{1,0:T(8,128)(2,1)S(1)}, bf16[512,256]{1,0:T(8,128)(2,1)S...) custom-call(s32[5]{0:T(128)S(1)} %copy-done.21, ...), custom_call_target="tpu_custom_call" | custom-call | tf_op jit(solution)/shard_map/pallas_call | solution.py:787
  154.2 2.9 shard_map.294
  157.8 3.7 %collective-permute-done.25.refs_6_ = bf16[512,256]{1,0:T(8,128)(2,1)S(1)} collective-permute-done((bf16[512,256]{1,0:T(8,128)(2,1)S(1)}, bf16[512,256]{1,0:T(8,128)(2,1)S(1)}, u32[]{:S(2)}, u32[]{:S(2)}) %collective-permute-start.25) | collective-permute-done | bytes 262176 | tf_op jit(solution)/shard_map/ppermute | solution.py:858
  161.4 4.8 %collective-permute-done.26.refs_7_ = bf16[512,256]{1,0:T(8,128)(2,1)S(1)} collective-permute-done((bf16[512,256]{1,0:T(8,128)(2,1)S(1)}, bf16[512,256]{1,0:T(8,128)(2,1)S(1)}, u32[]{:S(2)}, u32[]{:S(2)}) %collective-permute-start.26) | collective-permute-done | bytes 262176 | tf_op jit(solution)/shard_map/ppermute | solution.py:858
  169.7 16.0 %shard_map.295 = (bf16[2048,768]{1,0:T(8,128)(2,1)S(1)}, f32[1,768]{1,0:T(1,128)S(1)}) custom-call(s32[5]{0:T(128)S(1)} %copy-done.21, s32[2]{0:T(128)S(1)} %pad_add_fusion.place.place_ref, bf16[512,768]{1,0:T(8,128)(2,1)S(1)} %add_convert_fusion.9.refs_0_, bf16[512,768]{1,0:T(8,128)(2,1)S(1)} %add_convert_fusion.8.refs_1_, ...), custom_call_target="tpu_custom_call" | custom-call | tf_op jit(solution)/shard_map/pallas_call | solution.py:430
  188.2 5.3 %collective-permute-done.32 = bf16[256,1024]{1,0:T(8,128)(2,1)S(1)} collective-permute-done((bf16[256,1024]{1,0:T(8,128)(2,1)S(1)}, bf16[256,1024]{1,0:T(8,128)(2,1)S(1)}, u32[]{:S(2)}, u32[]{:S(2)}) %collective-permute-start.32) | collective-permute-done | bytes 524320 | tf_op jit(solution)/shard_map/ppermute | solution.py:858
  197.1 4.7 %shard_map.296 = (bf16[192,1024]{1,0:T(8,128)(2,1)S(1)}, bf16[192,1024]{1,0:T(8,128)(2,1)S(1)}, bf16[192,1024]{1,0:T(8,128)(2,1)S(1)}, bf16[192,1024]{1,0:T(8,128)(2,1)S(1)}) custom-call(s32[2]{0:T(128)S(1)} %pad_add_fusion.place.place_ref, bf16[2048,768]{1,0:T(8,128)(2,1)S(1)} %get-tuple-element.177.refs_0_, ...), custom_call_target="tpu_custom_call" | custom-call | tf_op jit(solution)/shard_map/pallas_call | solution.py:626
  201.8 4.9 %collective-permute-start.36 = (bf16[192,1024]{1,0:T(8,128)(2,1)S(1)}, bf16[192,1024]{1,0:T(8,128)(2,1)S(1)}, u32[]{:S(2)}, u32[]{:S(2)}) collective-permute-start(bf16[192,1024]{1,0:T(8,128)(2,1)S(1)} %get-tuple-element.176), channel_id=1, source_target_pairs={{0,8},{4,12},{8,0},{12,4},{16,24},{20,28},{24,16},{28,20},{1,9},{5... | collective-permute-start | bytes 1179656 | tf_op jit(solution)/shard_map/ppermute | solution.py:858
  207.0 4.7 %shard_map.297 = (bf16[512,1024]{1,0:T(8,128)(2,1)S(1)}, bf16[512,1024]{1,0:T(8,128)(2,1)}, bf16[512,1024]{1,0:T(8,128)(2,1)S(1)}, bf16[512,1024]{1,0:T(8,128)(2,1)}, f32[8,1024]{1,0:T(8,128)S(1)}) custom-call(bf16[2048,768]{1,0:T(8,128)(2,1)S(1)} %get-tuple-element.177.refs_0_, bf16[768,1024]{1,0:T(8,128)(2,1)S(1)} %bitcast.70, ...), custom_call_target="tpu_custom_call" | custom-call | tf_op jit(solution)/shard_map/pallas_call | solution.py:741
  212.9 10.0 %collective-permute-done.36 = bf16[192,1024]{1,0:T(8,128)(2,1)S(1)} collective-permute-done((bf16[192,1024]{1,0:T(8,128)(2,1)S(1)}, bf16[192,1024]{1,0:T(8,128)(2,1)S(1)}, u32[]{:S(2)}, u32[]{:S(2)}) %collective-permute-start.36) | collective-permute-done | bytes 393248 | tf_op jit(solution)/shard_map/ppermute | solution.py:858
  227.7 2.9 shard_map.298
  232.3 5.9 %collective-permute-start.45 = (bf16[256,1024]{1,0:T(8,128)(2,1)}, bf16[256,1024]{1,0:T(8,128)(2,1)}, u32[]{:S(2)}, u32[]{:S(2)}) collective-permute-start(bf16[256,1024]{1,0:T(8,128)(2,1)} %add_convert_fusion.10), channel_id=1, source_target_pairs={{0,16},{4,20},{8,24},{12,28},{16,0},{20,4},{24,8},{28,12},{1,17},{... | collective-permute-start | bytes 1572872 | tf_op jit(solution)/shard_map/ppermute | solution.py:858
  239.5 1.9 add_convert_fusion.1.half_a
  244.7 19.8 %collective-permute-done.46 = bf16[160,1024]{1,0:T(8,128)(2,1)S(1)} collective-permute-done((bf16[160,1024]{1,0:T(8,128)(2,1)}, bf16[160,1024]{1,0:T(8,128)(2,1)S(1)}, u32[]{:S(2)}, u32[]{:S(2)}) %collective-permute-start.46) | collective-permute-done | bytes 327712 | tf_op jit(solution)/shard_map/ppermute | solution.py:858
  271.9 4.7 %collective-permute-start.52 = (bf16[96,1024]{1,0:T(8,128)(2,1)S(1)}, bf16[96,1024]{1,0:T(8,128)(2,1)S(1)}, u32[]{:S(2)}, u32[]{:S(2)}) collective-permute-start(bf16[96,1024]{1,0:T(8,128)(2,1)S(1)} %pad_maximum_fusion.9), channel_id=1, source_target_pairs={{0,16},{4,20},{8,24},{12,28},{16,0},{20,4},{24,8},{28,12},{1,17},{... | collective-permute-start | bytes 589832 | tf_op jit(solution)/shard_map/ppermute | solution.py:858
  276.8 2.5 shard_map.299
  279.3 2.9 collective-permute-start.49
  282.2 16.4 %collective-permute-done.52 = bf16[96,1024]{1,0:T(8,128)(2,1)S(1)} collective-permute-done((bf16[96,1024]{1,0:T(8,128)(2,1)S(1)}, bf16[96,1024]{1,0:T(8,128)(2,1)S(1)}, u32[]{:S(2)}, u32[]{:S(2)}) %collective-permute-start.52) | collective-permute-done | bytes 196640 | tf_op jit(solution)/shard_map/ppermute | solution.py:858
  298.6 5.3 %collective-permute-done.51 = bf16[160,1024]{1,0:T(8,128)(2,1)S(1)} collective-permute-done((bf16[160,1024]{1,0:T(8,128)(2,1)S(1)}, bf16[160,1024]{1,0:T(8,128)(2,1)S(1)}, u32[]{:S(2)}, u32[]{:S(2)}) %collective-permute-start.51) | collective-permute-done | bytes 327712 | tf_op jit(solution)/shard_map/ppermute | solution.py:858
  304.0 7.2 %collective-permute-start.55 = (bf16[160,1024]{1,0:T(8,128)(2,1)S(1)}, bf16[160,1024]{1,0:T(8,128)(2,1)S(1)}, u32[]{:S(2)}, u32[]{:S(2)}) collective-permute-start(bf16[160,1024]{1,0:T(8,128)(2,1)S(1)} %add_convert_fusion.19), channel_id=1, source_target_pairs={{0,8},{4,12},{8,0},{12,4},{16,24},{20,28},{24,16},{28,20},{1,9},{5... | collective-permute-start | bytes 983048 | tf_op jit(solution)/shard_map/ppermute | solution.py:858
  312.8 2.8 shard_map.300
  315.7 2.8 shard_map.301
  320.4 3.3 collective-permute-done.54
  328.1 2.5 fusion.8
  331.2 2.2 collective-permute-done.58.refs_3_
  333.4 2.8 shard_map.302
  (236 shorter events, 75.9 us)
Async XLA Ops:
  0.7 32.1 %collective-permute-start.8 = (bf16[256,1024]{1,0:T(8,128)(2,1)}, bf16[256,1024]{1,0:T(8,128)(2,1)S(1)}, u32[]{:S(2)}, u32[]{:S(2)}) collective-permute-start(bf16[256,1024]{1,0:T(8,128)(2,1)} %refs_0_.1), channel_id=1, source_target_pairs={{0,1},{1,0},{2,3},{3,2},{4,5},{5,4},{6,7},{7,6},{8,9},{9,8},{10,11... | collective-permute-start | bytes 1572872 | tf_op jit(solution)/shard_map/ppermute | solution.py:858
  2.1 5.9 %collective-permute-start = (bf16[32,1024]{1,0:T(8,128)(2,1)S(1)}, bf16[32,1024]{1,0:T(8,128)(2,1)S(1)}, u32[]{:S(2)}, u32[]{:S(2)}) collective-permute-start(bf16[32,1024]{1,0:T(8,128)(2,1)S(1)} %constant_dynamic-slice_fusion), channel_id=1, source_target_pairs={{0,2},{1,3},{2,0},{3,1},{4,6},{5,7},{6,4},{7,5},{8,10},{9,11},{10,... | collective-permute-start | bytes 196616 | tf_op jit(solution)/shard_map/ppermute | solution.py:858
  7.3 25.6 %collective-permute-start.7 = (bf16[512,1024]{1,0:T(8,128)(2,1)S(1)}, bf16[512,1024]{1,0:T(8,128)(2,1)S(1)}, u32[]{:S(2)}, u32[]{:S(2)}) collective-permute-start(bf16[512,1024]{1,0:T(8,128)(2,1)S(1)} %shard_map.281.grad_mlp.refs_2_), channel_id=1, source_target_pairs={{0,1},{1,0},{2,3},{3,2},{4,5},{5,4},{6,7},{7,6},{8,9},{9,8},{10,11... | collective-permute-start | bytes 3145736 | tf_op jit(solution)/shard_map/ppermute | solution.py:858
  7.6 8.0 %collective-permute-start.2 = (bf16[64,1024]{1,0:T(8,128)(2,1)S(1)}, bf16[64,1024]{1,0:T(8,128)(2,1)S(1)}, u32[]{:S(2)}, u32[]{:S(2)}) collective-permute-start(bf16[64,1024]{1,0:T(8,128)(2,1)S(1)} %slice.278), channel_id=1, source_target_pairs={{0,2},{1,3},{2,0},{3,1},{4,6},{5,7},{6,4},{7,5},{8,10},{9,11},{10,... | collective-permute-start | bytes 393224 | tf_op jit(solution)/shard_map/ppermute | solution.py:858
  12.5 19.3 %collective-permute-start.1 = (bf16[512,1024]{1,0:T(8,128)(2,1)S(1)}, bf16[512,1024]{1,0:T(8,128)(2,1)S(1)}, u32[]{:S(2)}, u32[]{:S(2)}) collective-permute-start(bf16[512,1024]{1,0:T(8,128)(2,1)S(1)} %get-tuple-element.120.refs_1_.refs_2_), channel_id=1, source_target_pairs={{0,1},{1,0},{2,3},{3,2},{4,5},{5,4},{6,7},{7,6},{8,9},{9,8},{10,11... | collective-permute-start | bytes 3145736 | tf_op jit(solution)/shard_map/ppermute | solution.py:858
  12.7 7.0 %collective-permute-start.4 = (bf16[32,1024]{1,0:T(8,128)(2,1)S(1)}, bf16[32,1024]{1,0:T(8,128)(2,1)S(1)}, u32[]{:S(2)}, u32[]{:S(2)}) collective-permute-start(bf16[32,1024]{1,0:T(8,128)(2,1)S(1)} %collective-permute-done), channel_id=1, source_target_pairs={{0,16},{4,20},{8,24},{12,28},{16,0},{20,4},{24,8},{28,12},{1,17},{... | collective-permute-start | bytes 196616 | tf_op jit(solution)/shard_map/ppermute | solution.py:858
  15.6 25.3 %collective-permute-start.3 = (bf16[512,1024]{1,0:T(8,128)(2,1)S(1)}, bf16[512,1024]{1,0:T(8,128)(2,1)S(1)}, u32[]{:S(2)}, u32[]{:S(2)}) collective-permute-start(bf16[512,1024]{1,0:T(8,128)(2,1)S(1)} %get-tuple-element.120.refs_1_.refs_2_), channel_id=1, source_target_pairs={{0,2},{1,3},{2,0},{3,1},{4,6},{5,7},{6,4},{7,5},{8,10},{9,11},{10,... | collective-permute-start | bytes 3145736 | tf_op jit(solution)/shard_map/ppermute | solution.py:858
  24.7 6.5 %collective-permute-start.6 = (bf16[128,1024]{1,0:T(8,128)(2,1)S(1)}, bf16[128,1024]{1,0:T(8,128)(2,1)S(1)}, u32[]{:S(2)}, u32[]{:S(2)}) collective-permute-start(bf16[128,1024]{1,0:T(8,128)(2,1)S(1)} %constant_dynamic-update-slice_fusion.first), channel_id=1, source_target_pairs={{0,4},{4,0},{8,12},{12,8},{16,20},{20,16},{24,28},{28,24},{1,5},{5... | collective-permute-start | bytes 786440 | tf_op jit(solution)/shard_map/ppermute | solution.py:858
  40.9 22.8 %collective-permute-start.10 = (bf16[448,1024]{1,0:T(8,128)(2,1)S(1)}, bf16[448,1024]{1,0:T(8,128)(2,1)S(1)}, u32[]{:S(2)}, u32[]{:S(2)}) collective-permute-start(bf16[448,1024]{1,0:T(8,128)(2,1)S(1)} %slice.279), channel_id=1, source_target_pairs={{0,2},{1,3},{2,0},{3,1},{4,6},{5,7},{6,4},{7,5},{8,10},{9,11},{10,... | collective-permute-start | bytes 2752520 | tf_op jit(solution)/shard_map/ppermute | solution.py:858
  64.5 8.4 %collective-permute-start.14 = (bf16[512,256]{1,0:T(8,128)(2,1)S(1)}, bf16[512,256]{1,0:T(8,128)(2,1)S(1)}, u32[]{:S(2)}, u32[]{:S(2)}) collective-permute-start(bf16[512,256]{1,0:T(8,128)(2,1)S(1)} %get-tuple-element.236), channel_id=1, source_target_pairs={{0,3},{1,2},{2,1},{3,0},{4,7},{5,6},{6,5},{7,4},{8,11},{9,10},{10,... | collective-permute-start | bytes 786440 | tf_op jit(solution)/shard_map/ppermute | solution.py:858
  65.7 13.0 %collective-permute-start.13 = (bf16[512,256]{1,0:T(8,128)(2,1)S(1)}, bf16[512,256]{1,0:T(8,128)(2,1)S(1)}, u32[]{:S(2)}, u32[]{:S(2)}) collective-permute-start(bf16[512,256]{1,0:T(8,128)(2,1)S(1)} %get-tuple-element.237), channel_id=1, source_target_pairs={{0,2},{1,3},{2,0},{3,1},{4,6},{5,7},{6,4},{7,5},{8,10},{9,11},{10,... | collective-permute-start | bytes 786440 | tf_op jit(solution)/shard_map/ppermute | solution.py:858
  66.2 12.5 %collective-permute-start.12 = (bf16[512,256]{1,0:T(8,128)(2,1)S(1)}, bf16[512,256]{1,0:T(8,128)(2,1)S(1)}, u32[]{:S(2)}, u32[]{:S(2)}) collective-permute-start(bf16[512,256]{1,0:T(8,128)(2,1)S(1)} %get-tuple-element.238), channel_id=1, source_target_pairs={{0,1},{1,0},{2,3},{3,2},{4,5},{5,4},{6,7},{7,6},{8,9},{9,8},{10,11... | collective-permute-start | bytes 786440 | tf_op jit(solution)/shard_map/ppermute | solution.py:858
  82.2 25.6 %collective-permute-start.18 = (bf16[512,1024]{1,0:T(8,128)(2,1)S(1)}, bf16[512,1024]{1,0:T(8,128)(2,1)S(1)}, u32[]{:S(2)}, u32[]{:S(2)}) collective-permute-start(bf16[512,1024]{1,0:T(8,128)(2,1)S(1)} %get-tuple-element.128.normed.refs_0_), channel_id=1, source_target_pairs={{0,2},{1,3},{2,0},{3,1},{4,6},{5,7},{6,4},{7,5},{8,10},{9,11},{10,... | collective-permute-start | bytes 3145736 | tf_op jit(solution)/shard_map/ppermute | solution.py:858
  90.7 17.1 %collective-permute-start.20 = (bf16[512,1024]{1,0:T(8,128)(2,1)}, bf16[512,1024]{1,0:T(8,128)(2,1)}, u32[]{:S(2)}, u32[]{:S(2)}) collective-permute-start(bf16[512,1024]{1,0:T(8,128)(2,1)} %get-tuple-element.138), channel_id=1, source_target_pairs={{0,1},{1,0},{2,3},{3,2},{4,5},{5,4},{6,7},{7,6},{8,9},{9,8},{10,11... | collective-permute-start | bytes 3145736 | tf_op jit(solution)/shard_map/ppermute | solution.py:858
  90.9 18.5 %collective-permute-start.17 = (bf16[512,1024]{1,0:T(8,128)(2,1)S(1)}, bf16[512,1024]{1,0:T(8,128)(2,1)}, u32[]{:S(2)}, u32[]{:S(2)}) collective-permute-start(bf16[512,1024]{1,0:T(8,128)(2,1)S(1)} %get-tuple-element.130), channel_id=1, source_target_pairs={{0,1},{1,0},{2,3},{3,2},{4,5},{5,4},{6,7},{7,6},{8,9},{9,8},{10,11... | collective-permute-start | bytes 3145736 | tf_op jit(solution)/shard_map/ppermute | solution.py:858
  121.5 25.1 %collective-permute-start.23 = (bf16[512,1024]{1,0:T(8,128)(2,1)S(1)}, bf16[512,1024]{1,0:T(8,128)(2,1)S(1)}, u32[]{:S(2)}, u32[]{:S(2)}) collective-permute-start(bf16[512,1024]{1,0:T(8,128)(2,1)S(1)} %add_convert_fusion.3), channel_id=1, source_target_pairs={{0,2},{1,3},{2,0},{3,1},{4,6},{5,7},{6,4},{7,5},{8,10},{9,11},{10,... | collective-permute-start | bytes 3145736 | tf_op jit(solution)/shard_map/ppermute | solution.py:858
  130.7 26.5 %collective-permute-start.30 = (bf16[512,1024]{1,0:T(8,128)(2,1)S(1)}, bf16[512,1024]{1,0:T(8,128)(2,1)S(1)}, u32[]{:S(2)}, u32[]{:S(2)}) collective-permute-start(bf16[512,1024]{1,0:T(8,128)(2,1)S(1)} %get-tuple-element.150), channel_id=1, source_target_pairs={{0,8},{4,12},{8,0},{12,4},{16,24},{20,28},{24,16},{28,20},{1,9},{5... | collective-permute-start | bytes 3145736 | tf_op jit(solution)/shard_map/ppermute | solution.py:858
  132.4 33.9 %collective-permute-start.22 = (bf16[512,1024]{1,0:T(8,128)(2,1)S(1)}, bf16[512,1024]{1,0:T(8,128)(2,1)S(1)}, u32[]{:S(2)}, u32[]{:S(2)}) collective-permute-start(bf16[512,1024]{1,0:T(8,128)(2,1)S(1)} %get-tuple-element.145), channel_id=1, source_target_pairs={{0,4},{4,0},{8,12},{12,8},{16,20},{20,16},{24,28},{28,24},{1,5},{5... | collective-permute-start | bytes 3145736 | tf_op jit(solution)/shard_map/ppermute | solution.py:858
  152.3 9.1 %collective-permute-start.25 = (bf16[512,256]{1,0:T(8,128)(2,1)S(1)}, bf16[512,256]{1,0:T(8,128)(2,1)S(1)}, u32[]{:S(2)}, u32[]{:S(2)}) collective-permute-start(bf16[512,256]{1,0:T(8,128)(2,1)S(1)} %get-tuple-element.157), channel_id=1, source_target_pairs={{0,2},{1,3},{2,0},{3,1},{4,6},{5,7},{6,4},{7,5},{8,10},{9,11},{10,... | collective-permute-start | bytes 786440 | tf_op jit(solution)/shard_map/ppermute | solution.py:858
  153.8 12.5 %collective-permute-start.26 = (bf16[512,256]{1,0:T(8,128)(2,1)S(1)}, bf16[512,256]{1,0:T(8,128)(2,1)S(1)}, u32[]{:S(2)}, u32[]{:S(2)}) collective-permute-start(bf16[512,256]{1,0:T(8,128)(2,1)S(1)} %get-tuple-element.158), channel_id=1, source_target_pairs={{0,3},{1,2},{2,1},{3,0},{4,7},{5,6},{6,5},{7,4},{8,11},{9,10},{10,... | collective-permute-start | bytes 786440 | tf_op jit(solution)/shard_map/ppermute | solution.py:858
  157.2 28.5 %collective-permute-start.37 = (bf16[512,1024]{1,0:T(8,128)(2,1)S(1)}, bf16[512,1024]{1,0:T(8,128)(2,1)S(1)}, u32[]{:S(2)}, u32[]{:S(2)}) collective-permute-start(bf16[512,1024]{1,0:T(8,128)(2,1)S(1)} %convolution_convert_fusion), channel_id=1, source_target_pairs={{0,1},{1,0},{2,3},{3,2},{4,5},{5,4},{6,7},{7,6},{8,9},{9,8},{10,11... | collective-permute-start | bytes 3145736 | tf_op jit(solution)/shard_map/ppermute | solution.py:858
  157.5 11.7 %collective-permute-start.28 = (bf16[256,1024]{1,0:T(8,128)(2,1)S(1)}, bf16[256,1024]{1,0:T(8,128)(2,1)S(1)}, u32[]{:S(2)}, u32[]{:S(2)}) collective-permute-start(bf16[256,1024]{1,0:T(8,128)(2,1)S(1)} %get-tuple-element.162), channel_id=1, source_target_pairs={{0,1},{1,0},{2,3},{3,2},{4,5},{5,4},{6,7},{7,6},{8,9},{9,8},{10,11... | collective-permute-start | bytes 1572872 | tf_op jit(solution)/shard_map/ppermute | solution.py:858
  161.4 8.0 %collective-permute-start.29 = (bf16[256,1024]{1,0:T(8,128)(2,1)S(1)}, bf16[256,1024]{1,0:T(8,128)(2,1)S(1)}, u32[]{:S(2)}, u32[]{:S(2)}) collective-permute-start(bf16[256,1024]{1,0:T(8,128)(2,1)S(1)} %get-tuple-element.164), channel_id=1, source_target_pairs={{0,1},{1,0},{2,3},{3,2},{4,5},{5,4},{6,7},{7,6},{8,9},{9,8},{10,11... | collective-permute-start | bytes 1572872 | tf_op jit(solution)/shard_map/ppermute | solution.py:858
  167.3 26.3 %collective-permute-start.32 = (bf16[256,1024]{1,0:T(8,128)(2,1)S(1)}, bf16[256,1024]{1,0:T(8,128)(2,1)S(1)}, u32[]{:S(2)}, u32[]{:S(2)}) collective-permute-start(bf16[256,1024]{1,0:T(8,128)(2,1)S(1)} %get-tuple-element.226), channel_id=1, source_target_pairs={{0,16},{4,20},{8,24},{12,28},{16,0},{20,4},{24,8},{28,12},{1,17},{... | collective-permute-start | bytes 1572872 | tf_op jit(solution)/shard_map/ppermute | solution.py:858
  167.6 26.1 %collective-permute-start.27 = (bf16[256,1024]{1,0:T(8,128)(2,1)S(1)}, bf16[256,1024]{1,0:T(8,128)(2,1)S(1)}, u32[]{:S(2)}, u32[]{:S(2)}) collective-permute-start(bf16[256,1024]{1,0:T(8,128)(2,1)S(1)} %get-tuple-element.258), channel_id=1, source_target_pairs={{0,8},{4,12},{8,0},{12,4},{16,24},{20,28},{24,16},{28,20},{1,9},{5... | collective-permute-start | bytes 1572872 | tf_op jit(solution)/shard_map/ppermute | solution.py:858
  186.1 20.5 %collective-permute-start.33 = (bf16[256,1024]{1,0:T(8,128)(2,1)S(1)}, bf16[256,1024]{1,0:T(8,128)(2,1)S(1)}, u32[]{:S(2)}, u32[]{:S(2)}) collective-permute-start(bf16[256,1024]{1,0:T(8,128)(2,1)S(1)} %add_convert_fusion.15), channel_id=1, source_target_pairs={{0,2},{1,3},{2,0},{3,1},{4,6},{5,7},{6,4},{7,5},{8,10},{9,11},{10,... | collective-permute-start | bytes 1572872 | tf_op jit(solution)/shard_map/ppermute | solution.py:858
  187.7 40.0 %collective-permute-start.38 = (bf16[512,1024]{1,0:T(8,128)(2,1)S(1)}, bf16[512,1024]{1,0:T(8,128)(2,1)S(1)}, u32[]{:S(2)}, u32[]{:S(2)}) collective-permute-start(bf16[512,1024]{1,0:T(8,128)(2,1)S(1)} %add_convert_fusion.2), channel_id=1, source_target_pairs={{0,2},{1,3},{2,0},{3,1},{4,6},{5,7},{6,4},{7,5},{8,10},{9,11},{10,... | collective-permute-start | bytes 3145736 | tf_op jit(solution)/shard_map/ppermute | solution.py:858
  193.8 30.0 %collective-permute-start.34 = (bf16[256,1024]{1,0:T(8,128)(2,1)S(1)}, bf16[256,1024]{1,0:T(8,128)(2,1)S(1)}, u32[]{:S(2)}, u32[]{:S(2)}) collective-permute-start(bf16[256,1024]{1,0:T(8,128)(2,1)S(1)} %pad_maximum_fusion.5), channel_id=1, source_target_pairs={{0,4},{4,0},{8,12},{12,8},{16,20},{20,16},{24,28},{28,24},{1,5},{5... | collective-permute-start | bytes 1572872 | tf_op jit(solution)/shard_map/ppermute | solution.py:858
  195.6 28.7 %collective-permute-start.31 = (bf16[256,1024]{1,0:T(8,128)(2,1)S(1)}, bf16[256,1024]{1,0:T(8,128)(2,1)S(1)}, u32[]{:S(2)}, u32[]{:S(2)}) collective-permute-start(bf16[256,1024]{1,0:T(8,128)(2,1)S(1)} %pad_maximum_fusion.4), channel_id=1, source_target_pairs={{0,16},{4,20},{8,24},{12,28},{16,0},{20,4},{24,8},{28,12},{1,17},{... | collective-permute-start | bytes 1572872 | tf_op jit(solution)/shard_map/ppermute | solution.py:858
  201.8 21.1 %collective-permute-start.36 = (bf16[192,1024]{1,0:T(8,128)(2,1)S(1)}, bf16[192,1024]{1,0:T(8,128)(2,1)S(1)}, u32[]{:S(2)}, u32[]{:S(2)}) collective-permute-start(bf16[192,1024]{1,0:T(8,128)(2,1)S(1)} %get-tuple-element.176), channel_id=1, source_target_pairs={{0,8},{4,12},{8,0},{12,4},{16,24},{20,28},{24,16},{28,20},{1,9},{5... | collective-permute-start | bytes 1179656 | tf_op jit(solution)/shard_map/ppermute | solution.py:858
  211.7 14.9 %collective-permute-start.35 = (bf16[320,1024]{1,0:T(8,128)(2,1)S(1)}, bf16[320,1024]{1,0:T(8,128)(2,1)S(1)}, u32[]{:S(2)}, u32[]{:S(2)}) collective-permute-start(bf16[320,1024]{1,0:T(8,128)(2,1)S(1)} %bitcast.84), channel_id=1, source_target_pairs={{0,4},{4,0},{8,12},{12,8},{16,20},{20,16},{24,28},{28,24},{1,5},{5... | collective-permute-start | bytes 1966088 | tf_op jit(solution)/shard_map/ppermute | solution.py:858
  222.9 15.4 %collective-permute-start.39 = (bf16[512,1024]{1,0:T(8,128)(2,1)}, bf16[512,1024]{1,0:T(8,128)(2,1)}, u32[]{:S(2)}, u32[]{:S(2)}) collective-permute-start(bf16[512,1024]{1,0:T(8,128)(2,1)} %get-tuple-element.188), channel_id=1, source_target_pairs={{0,1},{1,0},{2,3},{3,2},{4,5},{5,4},{6,7},{7,6},{8,9},{9,8},{10,11... | collective-permute-start | bytes 3145736 | tf_op jit(solution)/shard_map/ppermute | solution.py:858
  223.8 14.6 %collective-permute-start.40 = (bf16[512,1024]{1,0:T(8,128)(2,1)}, bf16[512,1024]{1,0:T(8,128)(2,1)}, u32[]{:S(2)}, u32[]{:S(2)}) collective-permute-start(bf16[512,1024]{1,0:T(8,128)(2,1)} %get-tuple-element.191), channel_id=1, source_target_pairs={{0,1},{1,0},{2,3},{3,2},{4,5},{5,4},{6,7},{7,6},{8,9},{9,8},{10,11... | collective-permute-start | bytes 3145736 | tf_op jit(solution)/shard_map/ppermute | solution.py:858
  230.7 14.0 %collective-permute-start.47 = (bf16[96,1024]{1,0:T(8,128)(2,1)}, bf16[96,1024]{1,0:T(8,128)(2,1)}, u32[]{:S(2)}, u32[]{:S(2)}) collective-permute-start(bf16[96,1024]{1,0:T(8,128)(2,1)} %get-tuple-element.240), channel_id=1, source_target_pairs={{0,4},{4,0},{8,12},{12,8},{16,20},{20,16},{24,28},{28,24},{1,5},{5... | collective-permute-start | bytes 589832 | tf_op jit(solution)/shard_map/ppermute | solution.py:858
  232.0 32.5 %collective-permute-start.44 = (bf16[256,1024]{1,0:T(8,128)(2,1)}, bf16[256,1024]{1,0:T(8,128)(2,1)}, u32[]{:S(2)}, u32[]{:S(2)}) collective-permute-start(bf16[256,1024]{1,0:T(8,128)(2,1)} %add_convert_fusion.11), channel_id=1, source_target_pairs={{0,8},{4,12},{8,0},{12,4},{16,24},{20,28},{24,16},{28,20},{1,9},{5... | collective-permute-start | bytes 1572872 | tf_op jit(solution)/shard_map/ppermute | solution.py:858
  232.3 32.2 %collective-permute-start.45 = (bf16[256,1024]{1,0:T(8,128)(2,1)}, bf16[256,1024]{1,0:T(8,128)(2,1)}, u32[]{:S(2)}, u32[]{:S(2)}) collective-permute-start(bf16[256,1024]{1,0:T(8,128)(2,1)} %add_convert_fusion.10), channel_id=1, source_target_pairs={{0,16},{4,20},{8,24},{12,28},{16,0},{20,4},{24,8},{28,12},{1,17},{... | collective-permute-start | bytes 1572872 | tf_op jit(solution)/shard_map/ppermute | solution.py:858
  238.3 26.2 %collective-permute-start.46 = (bf16[160,1024]{1,0:T(8,128)(2,1)}, bf16[160,1024]{1,0:T(8,128)(2,1)S(1)}, u32[]{:S(2)}, u32[]{:S(2)}) collective-permute-start(bf16[160,1024]{1,0:T(8,128)(2,1)} %get-tuple-element.230), channel_id=1, source_target_pairs={{0,8},{4,12},{8,0},{12,4},{16,24},{20,28},{24,16},{28,20},{1,9},{5... | collective-permute-start | bytes 983048 | tf_op jit(solution)/shard_map/ppermute | solution.py:858
  243.1 33.5 %collective-permute-start.41 = (bf16[512,1024]{1,0:T(8,128)(2,1)S(1)}, bf16[512,1024]{1,0:T(8,128)(2,1)S(1)}, u32[]{:S(2)}, u32[]{:S(2)}) collective-permute-start(bf16[512,1024]{1,0:T(8,128)(2,1)S(1)} %add_convert_fusion), channel_id=1, source_target_pairs={{0,2},{1,3},{2,0},{3,1},{4,6},{5,7},{6,4},{7,5},{8,10},{9,11},{10,... | collective-permute-start | bytes 3145736 | tf_op jit(solution)/shard_map/ppermute | solution.py:858
  264.5 14.8 %collective-permute-start.48 = (f32[80,128]{1,0:T(8,128)S(1)}, f32[80,128]{1,0:T(8,128)S(1)}, u32[]{:S(2)}, u32[]{:S(2)}) collective-permute-start(f32[80,128]{1,0:T(8,128)S(1)} %slice.292), channel_id=1, source_target_pairs={{0,2},{1,3},{2,0},{3,1},{4,6},{5,7},{6,4},{7,5},{8,10},{9,11},{10,... | collective-permute-start | bytes 122888 | tf_op jit(solution)/shard_map/ppermute | solution.py:858
  267.3 45.5 %collective-permute-start.50 = (bf16[512,1024]{1,0:T(8,128)(2,1)S(1)}, bf16[512,1024]{1,0:T(8,128)(2,1)S(1)}, u32[]{:S(2)}, u32[]{:S(2)}) collective-permute-start(bf16[512,1024]{1,0:T(8,128)(2,1)S(1)} %pad_maximum_fusion.first), channel_id=1, source_target_pairs={{0,4},{4,0},{8,12},{12,8},{16,20},{20,16},{24,28},{28,24},{1,5},{5... | collective-permute-start | bytes 3145736 | tf_op jit(solution)/shard_map/ppermute | solution.py:858
  269.3 43.5 %collective-permute-start.53 = (bf16[512,1024]{1,0:T(8,128)(2,1)S(1)}, bf16[512,1024]{1,0:T(8,128)(2,1)S(1)}, u32[]{:S(2)}, u32[]{:S(2)}) collective-permute-start(bf16[512,1024]{1,0:T(8,128)(2,1)S(1)} %pad_maximum_fusion.1.first), channel_id=1, source_target_pairs={{0,8},{4,12},{8,0},{12,4},{16,24},{20,28},{24,16},{28,20},{1,9},{5... | collective-permute-start | bytes 3145736 | tf_op jit(solution)/shard_map/ppermute | solution.py:858
  271.9 26.7 %collective-permute-start.52 = (bf16[96,1024]{1,0:T(8,128)(2,1)S(1)}, bf16[96,1024]{1,0:T(8,128)(2,1)S(1)}, u32[]{:S(2)}, u32[]{:S(2)}) collective-permute-start(bf16[96,1024]{1,0:T(8,128)(2,1)S(1)} %pad_maximum_fusion.9), channel_id=1, source_target_pairs={{0,16},{4,20},{8,24},{12,28},{16,0},{20,4},{24,8},{28,12},{1,17},{... | collective-permute-start | bytes 589832 | tf_op jit(solution)/shard_map/ppermute | solution.py:858
  276.7 27.2 %collective-permute-start.51 = (bf16[160,1024]{1,0:T(8,128)(2,1)S(1)}, bf16[160,1024]{1,0:T(8,128)(2,1)S(1)}, u32[]{:S(2)}, u32[]{:S(2)}) collective-permute-start(bf16[160,1024]{1,0:T(8,128)(2,1)S(1)} %pad_maximum_fusion.8), channel_id=1, source_target_pairs={{0,16},{4,20},{8,24},{12,28},{16,0},{20,4},{24,8},{28,12},{1,17},{... | collective-permute-start | bytes 983048 | tf_op jit(solution)/shard_map/ppermute | solution.py:858
  279.3 39.2 %collective-permute-start.49 = (f32[96,128]{1,0:T(8,128)S(1)}, f32[96,128]{1,0:T(8,128)S(1)}, u32[]{:S(2)}, u32[]{:S(2)}) collective-permute-start(f32[96,128]{1,0:T(8,128)S(1)} %pad_maximum_fusion.13), channel_id=1, source_target_pairs={{0,16},{4,20},{8,24},{12,28},{16,0},{20,4},{24,8},{28,12},{1,17},{... | collective-permute-start | bytes 147464 | tf_op jit(solution)/shard_map/ppermute | solution.py:858
  304.0 14.5 %collective-permute-start.55 = (bf16[160,1024]{1,0:T(8,128)(2,1)S(1)}, bf16[160,1024]{1,0:T(8,128)(2,1)S(1)}, u32[]{:S(2)}, u32[]{:S(2)}) collective-permute-start(bf16[160,1024]{1,0:T(8,128)(2,1)S(1)} %add_convert_fusion.19), channel_id=1, source_target_pairs={{0,8},{4,12},{8,0},{12,4},{16,24},{20,28},{24,16},{28,20},{1,9},{5... | collective-permute-start | bytes 983048 | tf_op jit(solution)/shard_map/ppermute | solution.py:858
  311.3 14.2 %collective-permute-start.57 = (bf16[96,1024]{1,0:T(8,128)(2,1)S(1)}, bf16[96,1024]{1,0:T(8,128)(2,1)S(1)}, u32[]{:S(2)}, u32[]{:S(2)}) collective-permute-start(bf16[96,1024]{1,0:T(8,128)(2,1)S(1)} %add_convert_fusion.24), channel_id=1, source_target_pairs={{0,4},{4,0},{8,12},{12,8},{16,20},{20,16},{24,28},{28,24},{1,5},{5... | collective-permute-start | bytes 589832 | tf_op jit(solution)/shard_map/ppermute | solution.py:858
  318.6 14.8 %collective-permute-start.56 = (bf16[320,1024]{1,0:T(8,128)(2,1)S(1)}, bf16[320,1024]{1,0:T(8,128)(2,1)S(1)}, u32[]{:S(2)}, u32[]{:S(2)}) collective-permute-start(bf16[320,1024]{1,0:T(8,128)(2,1)S(1)} %pad_maximum_fusion.3.refs_0_), channel_id=1, source_target_pairs={{0,4},{4,0},{8,12},{12,8},{16,20},{20,16},{24,28},{28,24},{1,5},{5... | collective-permute-start | bytes 1966088 | tf_op jit(solution)/shard_map/ppermute | solution.py:858
  325.6 7.8 %collective-permute-start.58 = (bf16[192,1024]{1,0:T(8,128)(2,1)S(1)}, bf16[192,1024]{1,0:T(8,128)(2,1)S(1)}, u32[]{:S(2)}, u32[]{:S(2)}) collective-permute-start(bf16[192,1024]{1,0:T(8,128)(2,1)S(1)} %pad_maximum_fusion.6.refs_2_), channel_id=1, source_target_pairs={{0,8},{4,12},{8,0},{12,4},{16,24},{20,28},{24,16},{28,20},{1,9},{5... | collective-permute-start | bytes 1179656 | tf_op jit(solution)/shard_map/ppermute | solution.py:858
  (44 other events, 373.4 us)
